TPU v7x, 128 devices: a whole 4x4x4 slice. The times are simulated.
128 devices in a mesh: row: 8 (over y_lo, x), col: 16 (over z, y_hi, core).
Axes of the slice: x: 4, y: 4 (y_hi: 2, y_lo: 2; y = y_hi * 2 + y_lo), z: 4, core: 2. Of those that a mesh axis runs over, the one named last changes fastest.
Arguments:
- hidden_in: bfloat16 [2048, 8192], P('col', 'row'), may hold values from -130 to 130
- norm_gain: float32 [8192], P('row'), may hold values from 0.5 to 1.5
- w_query: bfloat16 [8192, 8192], P('row', 'col'), may hold values from -0.0625 to 0.0625
- scale_query: float32 [64, 64], P('row', 'col'), may hold values from 0.35 to 2.8
- bias_query: float32 [8192], P('col'), may hold values from -14 to 14
- w_keyval: bfloat16 [8192, 2048], P('row'), may hold values from -0.0625 to 0.0625
- scale_keyval: float32 [64, 16], P('row'), may hold values from 0.35 to 2.8
- bias_keyval: float32 [2048], replicated, may hold values from -3 to 3
- w_out: bfloat16 [8192, 8192], P('col', 'row'), may hold values from -0.0625 to 0.0625
- scale_out: float32 [64, 64], P('col', 'row'), may hold values from 0.35 to 2.8
- cache_keyval: bfloat16 [2, 8192, 1024], P(None, 'row'), may hold values from -14 to 14
- span_offset: int32 [1], replicated, may hold values from 2048 to 8192
Outputs:
- hidden_out: bfloat16 [2048, 8192], P('col', 'row')
All inputs are finite; a program needn't handle non-finite values.
Results may differ from a plain program's by a relative error of at most 0.033.
Values may be sent and summed in bfloat16 or wider, within the bound.
No kernel may reach another device: no remote copies, remote signals or barrier semaphores. Data moves between devices by JAX's collectives and lax.ppermute only.
A program may use at most 192 MiB of HBM per device.

v0:
```python
import math

import jax
import jax.numpy as jnp
from jax import lax
from jax.sharding import PartitionSpec as P

D = 8192
H = 64
KVH = 8
HD = 128
QB = 128


EPSILON = 1e-06
ROPE_BASE = 1000000.0
MASKED = -1e30


def dequantize(weight, block_scale):
    expanded = jnp.repeat(jnp.repeat(block_scale, QB, axis=0), QB, axis=1)
    return (weight.astype(jnp.float32) * expanded).astype(jnp.bfloat16)


def rotate(vectors, positions):
    half_dim = HD // 2
    inverse = ROPE_BASE ** (-(2.0 * jnp.arange(half_dim, dtype=jnp.float32)) / HD)
    angles = positions[:, None] * inverse[None, :]
    cosine = jnp.cos(angles)[:, None, :]
    sine_part = jnp.sin(angles)[:, None, :]
    first_half = vectors[..., :half_dim]
    second = vectors[..., half_dim:]
    return jnp.concatenate(
        [first_half * cosine - second * sine_part, second * cosine + first_half * sine_part],
        axis=-1,
    )


def block_scores(queries, key_block, key_index, query_index, offset, cache_len):
    scores = jnp.einsum("thd,kd->htk", queries, key_block, preferred_element_type=jnp.float32) * (
        1.0 / math.sqrt(HD)
    )
    earlier = (key_index < cache_len)[None, :]
    allowed = jnp.where(
        earlier,
        (key_index < offset)[None, :],
        (key_index - cache_len)[None, :] <= query_index[:, None],
    )
    return jnp.where(allowed[None, :, :], scores, MASKED)


def score_blocks(queries, key_rows, key_index, query_index, offset, cache_len, block_len):
    key_blocks = key_rows.reshape(-1, block_len, key_rows.shape[-1])
    index_blocks = key_index.reshape(-1, block_len)

    def one_block(block_item):
        return block_scores(queries, block_item[0], block_item[1], query_index, offset, cache_len)

    return lax.map(one_block, (key_blocks, index_blocks))


def block_stats(scores):
    row_peak = jnp.max(scores, axis=(0, 3))
    weights = jnp.where(scores > 0.5 * MASKED, jnp.exp(scores - row_peak[None, :, :, None]), 0.0)
    return (row_peak, jnp.sum(weights, axis=(0, 3)))


def weighted_values(scores, value_rows, block_len, row_peak, row_total):
    value_blocks = value_rows.reshape(-1, block_len, value_rows.shape[-1])

    def advance(summed, block_item):
        weights = (jnp.exp(block_item[0] - row_peak[:, :, None]) / row_total[:, :, None]).astype(
            jnp.bfloat16
        )
        return (
            summed
            + jnp.einsum("htk,kd->thd", weights, block_item[1], preferred_element_type=jnp.float32),
            None,
        )

    start_state = jnp.zeros((scores.shape[2], scores.shape[1], HD), jnp.float32)
    return lax.scan(advance, start_state, (scores, value_blocks))[0]


def body(
    hidden_in,
    norm_gain,
    w_query,
    scale_query,
    bias_query,
    w_keyval,
    scale_keyval,
    bias_keyval,
    w_out,
    scale_out,
    cache_keyval,
    span_offset,
):
    row_count = lax.axis_size("row")
    row_index = lax.axis_index("row")
    col_index = lax.axis_index("col")
    widened = hidden_in.astype(jnp.float32)
    squares = lax.psum(jnp.sum(widened * widened, axis=1), "row")
    norm_ratio = lax.rsqrt(squares / D + EPSILON)
    normed = (widened * norm_ratio[:, None] * norm_gain[None, :]).astype(jnp.bfloat16)
    gathered = lax.all_gather(normed, "col", axis=0, tiled=True)
    tokens = gathered.shape[0]
    tok_dev = tokens // row_count
    heads_dev = w_query.shape[1] // HD
    qwidth = heads_dev * HD
    group_size = H // KVH
    kv_width = KVH * HD
    kv_head = col_index * heads_dev // group_size
    key_cols = lax.dynamic_slice_in_dim(w_keyval, kv_head * HD, HD, 1)
    value_cols = lax.dynamic_slice_in_dim(w_keyval, kv_width + kv_head * HD, HD, 1)
    key_scale = lax.dynamic_slice_in_dim(scale_keyval, kv_head * (HD // QB), HD // QB, 1)
    value_scale = lax.dynamic_slice_in_dim(
        scale_keyval, (kv_width + kv_head * HD) // QB, HD // QB, 1
    )
    combined = jnp.concatenate(
        [
            dequantize(w_query, scale_query),
            dequantize(key_cols, key_scale),
            dequantize(value_cols, value_scale),
        ],
        axis=1,
    )
    projected = lax.psum_scatter(
        jnp.dot(gathered, combined, preferred_element_type=jnp.float32).astype(jnp.bfloat16),
        "row",
        scatter_dimension=0,
        tiled=True,
    ).astype(jnp.float32)
    bias_key = lax.dynamic_slice_in_dim(bias_keyval, kv_head * HD, HD, 0)
    bias_value = lax.dynamic_slice_in_dim(bias_keyval, kv_width + kv_head * HD, HD, 0)
    offset = span_offset[0]
    query_index = row_index * tok_dev + jnp.arange(tok_dev, dtype=jnp.int32)
    positions = (offset + query_index).astype(jnp.float32)
    queries = rotate(
        (projected[:, :qwidth] + bias_query[None, :]).reshape(tok_dev, heads_dev, HD), positions
    ).astype(jnp.bfloat16)
    own_keys = rotate(
        (projected[:, qwidth : qwidth + HD] + bias_key[None, :]).reshape(tok_dev, 1, HD), positions
    )
    own_keys = own_keys.reshape(tok_dev, HD).astype(jnp.bfloat16)
    own_values = (projected[:, qwidth + HD :] + bias_value[None, :]).astype(jnp.bfloat16)
    span_kv = lax.all_gather(
        jnp.concatenate([own_keys, own_values], axis=1), "row", axis=0, tiled=True
    )
    span_keys = span_kv[:, :HD]
    span_values = span_kv[:, HD:]
    cache_dev = cache_keyval.shape[1]
    cache_len = cache_dev * row_count
    cache_head = lax.dynamic_slice_in_dim(cache_keyval, kv_head * HD, HD, 2)
    span_index = cache_len + jnp.arange(tokens, dtype=jnp.int32)
    all_queries = lax.all_gather(
        queries.reshape(tok_dev, qwidth), "row", axis=0, tiled=True
    ).reshape(tokens, heads_dev, HD)
    every_index = jnp.arange(tokens, dtype=jnp.int32)
    cache_index = row_index * cache_dev + jnp.arange(cache_dev, dtype=jnp.int32)
    cache_scores = score_blocks(
        all_queries, cache_head[0], cache_index, every_index, offset, cache_len, tok_dev
    )
    cache_peak, cache_total = block_stats(cache_scores)
    own_scores = score_blocks(
        queries, span_keys, span_index, query_index, offset, cache_len, tokens
    )
    own_peak, own_total = block_stats(own_scores)
    first_row = row_index * tok_dev
    placed_peak = lax.dynamic_update_slice_in_dim(
        jnp.full_like(cache_peak, MASKED), own_peak, first_row, 1
    )
    peak_all = lax.pmax(jnp.maximum(cache_peak, placed_peak).astype(jnp.bfloat16), "row").astype(
        jnp.float32
    )
    peak_own = lax.dynamic_slice_in_dim(peak_all, first_row, tok_dev, 1)
    placed_total = lax.dynamic_update_slice_in_dim(
        jnp.zeros_like(cache_total), own_total * jnp.exp(own_peak - peak_own), first_row, 1
    )
    total_all = lax.psum(
        (cache_total * jnp.exp(cache_peak - peak_all) + placed_total).astype(jnp.bfloat16), "row"
    ).astype(jnp.float32)
    total_own = lax.dynamic_slice_in_dim(total_all, first_row, tok_dev, 1)
    cache_part = weighted_values(cache_scores, cache_head[1], tok_dev, peak_all, total_all)
    cache_share = lax.psum_scatter(
        cache_part.reshape(tokens, qwidth).astype(jnp.bfloat16),
        "row",
        scatter_dimension=0,
        tiled=True,
    ).astype(jnp.float32)
    span_part = weighted_values(own_scores, span_values, tokens, peak_own, total_own)
    attended = cache_share.reshape(tok_dev, heads_dev, HD) + span_part
    attended = attended.reshape(tok_dev, qwidth).astype(jnp.bfloat16)
    attention_all = lax.all_gather(attended, "row", axis=0, tiled=True)
    out_weight = dequantize(w_out, scale_out)
    mixed_out = lax.psum_scatter(
        jnp.dot(attention_all, out_weight, preferred_element_type=jnp.float32).astype(jnp.bfloat16),
        "col",
        scatter_dimension=0,
        tiled=True,
    )
    return mixed_out


def solution(mesh):
    return jax.shard_map(
        body,
        mesh=mesh,
        in_specs=(
            P("col", "row"),
            P("row"),
            P("row", "col"),
            P("row", "col"),
            P("col"),
            P("row", None),
            P("row", None),
            P(),
            P("col", "row"),
            P("col", "row"),
            P(None, "row", None),
            P(),
        ),
        out_specs=P("col", "row"),
        check_vma=False,
    )
```

profile of v0, /device:TPU:0, one launch (start us, length us, event | category | flops | bytes accessed | tf_op | source)
XLA Modules:
  0.0 627.0 jit_solution(3063638257543192442)
XLA Ops:
  7.7 19.8 %psum.14 = f32[128]{0:T(128)S(1)} all-reduce(f32[128]{0:T(128)S(1)} %fusion.27), channel_id=1, replica_groups=mesh['row'=8,'col'=16] {'row'}, use_global_device_ids=true, to_apply=%region_1.0 | all-reduce | flops 128 | bytes 1024 | tf_op jit(solution)/shard_map/psum | solution.py:103
  34.3 50.2 %all-gather.5.cloned.1.call-done = bf16[2048,1024]{1,0:T(8,128)(2,1)} async-done(((bf16[128,1024]{1,0:T(8,128)(2,1)}), bf16[2048,1024]{1,0:T(8,128)(2,1)}) %all-gather.5.cloned.1.call-update) | async-done | bytes 4194320 | tf_op jit(solution)/shard_map/all_gather | solution.py:106
  84.6 7.2 %convolution_convert_fusion.1 = bf16[2048,768]{0,1:T(8,128)(2,1)} fusion(bf16[2048,1024]{1,0:T(8,128)(2,1)} %all-gather.5.cloned.1.call-done, bf16[1024,128]{1,0:T(8,128)(2,1)S(1)} %get-tuple-element.263, bf16[1024,128]{1,0:T(8,128)(2,1)S(1)} %get-tuple-element.262, bf16[1024,512]{1,0:T(8,128)(2,1)S(1)} %fusion.16), kind=kOutput, calls=%fused_computation.27 | convolution fusion | flops 3227516928 | bytes 8912896 | tf_op jit(solution)/shard_map/dot_general | solution.py:129
  93.3 42.3 %reduce-scatter.4.cloned.1.call-done = bf16[256,768]{0,1:T(8,128)(2,1)} async-done(((bf16[2048,768]{0,1:T(8,128)(2,1)}), bf16[256,768]{0,1:T(8,128)(2,1)}) %reduce-scatter.4.cloned.1.call-update) | async-done | bytes 393232 | tf_op jit(solution)/shard_map/reduce_scatter | solution.py:128
  143.1 31.9 %all-gather.9.cloned.1.call-done = bf16[2048,256]{0,1:T(8,128)(2,1)} async-done(((bf16[256,256]{0,1:T(8,128)(2,1)}), bf16[2048,256]{0,1:T(8,128)(2,1)}) %all-gather.9.cloned.1.call-update) | async-done | bytes 1048592 | tf_op jit(solution)/shard_map/all_gather | solution.py:147
  183.1 40.4 %all-gather.7.cloned.1.call-done = bf16[2048,512]{0,1:T(8,128)(2,1)} async-done(((bf16[256,512]{0,1:T(8,128)(2,1)}), bf16[2048,512]{0,1:T(8,128)(2,1)}) %all-gather.7.cloned.1.call-update) | async-done | bytes 2097168 | tf_op jit(solution)/shard_map/all_gather | solution.py:156
  226.6 24.4 %while.34 = (s32[]{:T(128)}, f32[4,4,2048,256]{2,3,1,0:T(8,128)}, s32[4,256]{1,0:T(4,128)S(1)}, s32[]{:T(128)}, bf16[4,256,128]{2,1,0:T(8,128)(2,1)S(1)}, /*index=5*/bf16[2048,4,128]{2,0,1:T(8,128)(2,1)S(1)}) while((s32[]{:T(128)}, f32[4,4,2048,256]{2,3,1,0:T(8,128)}, s32[4,256]{1,0:T(4,128)S(1)}, s32[]{:T(128)}, ...), condition=%wide.region_4.5_spmd.clone.clone, body=%wide.region_3.4_spmd.clone.sunk.clone | while | flops 542114560 | bytes 11606097 | solution.py:59
  227.9 4.8 bitcast_dynamic-update-slice_fusion.3
  234.0 4.8 bitcast_dynamic-update-slice_fusion.3
  240.1 4.8 bitcast_dynamic-update-slice_fusion.3
  250.9 12.0 %reduce_max.18 = f32[4,2048]{1,0:T(4,128)S(1)} reduce(f32[4,4,2048,256]{2,3,1,0:T(8,128)} %get-tuple-element.414, f32[]{:T(128)} %constant.145.clone.1), dimensions={0,3}, to_apply=%region_5.6 | reduce | flops 8380416 | bytes 33587204 | tf_op jit(solution)/shard_map/reduce_max | solution.py:63
  262.9 14.1 %select_reduce_fusion = f32[4,2048]{1,0:T(4,128)S(1)} fusion(f32[4,4,2048,256]{2,3,1,0:T(8,128)} %get-tuple-element.414, f32[4,2048]{1,0:T(4,128)S(1)} %reduce_max.18), kind=kLoop, calls=%fused_computation.20 | loop fusion | flops 33546240 | bytes 33619968 | tf_op jit(solution)/shard_map/reduce_sum | solution.py:65
  277.0 33.2 %pmax.7 = bf16[4,2048]{1,0:T(4,128)(2,1)S(1)} all-reduce(bf16[4,2048]{1,0:T(4,128)(2,1)S(1)} %max.7), channel_id=1, replica_groups=mesh['row'=8,'col'=16] {'row'}, use_global_device_ids=true, to_apply=%region_7.8 | all-reduce | flops 8192 | bytes 32768 | tf_op jit(solution)/shard_map/pmax | solution.py:173
  310.3 30.6 %psum.15 = bf16[4,2048]{1,0:T(4,128)(2,1)S(1)} all-reduce(bf16[4,2048]{1,0:T(4,128)(2,1)S(1)} %convert_element_type.113), channel_id=1, replica_groups=mesh['row'=8,'col'=16] {'row'}, use_global_device_ids=true, to_apply=%region_10.11 | all-reduce | flops 8192 | bytes 32768 | tf_op jit(solution)/shard_map/psum | solution.py:180
  340.9 95.2 %while.35 = (s32[]{:T(128)}, f32[2048,4,128]{0,2,1:T(8,128)}, bf16[4,256,128]{2,1,0:T(8,128)(2,1)S(1)}, f32[4,4,2048,256]{2,3,1,0:T(8,128)}, f32[4,2048]{1,0:T(4,128)S(1)}, /*index=5*/f32[4,2048]{1,0:T(4,128)S(1)}) while((s32[]{:T(128)}, f32[2048,4,128]{0,2,1:T(8,128)}, bf16[4,256,128]{2,1,0:T(8,128)(2,1)S(1)}, ...), condition=%wide.region_12.13_spmd.clone.clone, body=%wide.region_11.12_spmd.clone.sunk.clone | while | flops 545259520 | bytes 50462804 | solution.py:82
  340.9 7.7 %constant_dynamic-slice_fusion.8 = f32[1,4,2048,256]{2,3,1,0:T(8,128)} fusion(f32[4,4,2048,256]{2,3,1,0:T(8,128)} %get-tuple-element.426, s32[]{:T(128)} %get-tuple-element.417), kind=kLoop, calls=%fused_computation.7.clone.1.clone | loop fusion | bytes 16777220 | tf_op jit(solution)/shard_map/while/body/jit(dynamic_index_in_dim)/dynamic_slice | solution.py:82
  348.6 8.7 %copy.53 = f32[1,4,2048,256]{3,2,1,0:T(8,128)} copy(f32[1,4,2048,256]{2,3,1,0:T(8,128)} %constant_dynamic-slice_fusion.8) | data formatting | bytes 16777216 | tf_op jit(solution)/shard_map/while/body/jit(dynamic_index_in_dim)/dynamic_slice | solution.py:82
  357.3 6.8 %bitcast_add_fusion.3 = f32[2048,4,128]{0,2,1:T(8,128)} fusion(f32[2048,4,128]{0,2,1:T(8,128)} %get-tuple-element.418, f32[4,2048]{1,0:T(4,128)S(1)} %get-tuple-element.428, f32[1,4,2048,256]{3,2,1,0:T(8,128)} %copy.53, f32[4,2048]{1,0:T(4,128)S(1)} %get-tuple-element.427, pred[]{:T(512)S(6)} %compare.8, ...), kind=kOutput, calls=%fused_computation.2.clone.1.clone | convolution fusion | flops 545259520 | bytes 16908292 | tf_op jit(solution)/shard_map/while/body/eval_jaxpr/htk,kd->thd/dot_general | solution.py:77
  364.1 7.7 %constant_dynamic-slice_fusion.8 = f32[1,4,2048,256]{2,3,1,0:T(8,128)} fusion(f32[4,4,2048,256]{2,3,1,0:T(8,128)} %get-tuple-element.426, s32[]{:T(128)} %get-tuple-element.417), kind=kLoop, calls=%fused_computation.7.clone.1.clone | loop fusion | bytes 16777220 | tf_op jit(solution)/shard_map/while/body/jit(dynamic_index_in_dim)/dynamic_slice | solution.py:82
  371.8 8.7 %copy.53 = f32[1,4,2048,256]{3,2,1,0:T(8,128)} copy(f32[1,4,2048,256]{2,3,1,0:T(8,128)} %constant_dynamic-slice_fusion.8) | data formatting | bytes 16777216 | tf_op jit(solution)/shard_map/while/body/jit(dynamic_index_in_dim)/dynamic_slice | solution.py:82
  380.5 7.6 %bitcast_add_fusion.3 = f32[2048,4,128]{0,2,1:T(8,128)} fusion(f32[2048,4,128]{0,2,1:T(8,128)} %get-tuple-element.418, f32[4,2048]{1,0:T(4,128)S(1)} %get-tuple-element.428, f32[1,4,2048,256]{3,2,1,0:T(8,128)} %copy.53, f32[4,2048]{1,0:T(4,128)S(1)} %get-tuple-element.427, pred[]{:T(512)S(6)} %compare.8, ...), kind=kOutput, calls=%fused_computation.2.clone.1.clone | convolution fusion | flops 545259520 | bytes 16908292 | tf_op jit(solution)/shard_map/while/body/eval_jaxpr/htk,kd->thd/dot_general | solution.py:77
  388.1 7.7 %constant_dynamic-slice_fusion.8 = f32[1,4,2048,256]{2,3,1,0:T(8,128)} fusion(f32[4,4,2048,256]{2,3,1,0:T(8,128)} %get-tuple-element.426, s32[]{:T(128)} %get-tuple-element.417), kind=kLoop, calls=%fused_computation.7.clone.1.clone | loop fusion | bytes 16777220 | tf_op jit(solution)/shard_map/while/body/jit(dynamic_index_in_dim)/dynamic_slice | solution.py:82
  395.8 8.7 %copy.53 = f32[1,4,2048,256]{3,2,1,0:T(8,128)} copy(f32[1,4,2048,256]{2,3,1,0:T(8,128)} %constant_dynamic-slice_fusion.8) | data formatting | bytes 16777216 | tf_op jit(solution)/shard_map/while/body/jit(dynamic_index_in_dim)/dynamic_slice | solution.py:82
  404.5 7.6 %bitcast_add_fusion.3 = f32[2048,4,128]{0,2,1:T(8,128)} fusion(f32[2048,4,128]{0,2,1:T(8,128)} %get-tuple-element.418, f32[4,2048]{1,0:T(4,128)S(1)} %get-tuple-element.428, f32[1,4,2048,256]{3,2,1,0:T(8,128)} %copy.53, f32[4,2048]{1,0:T(4,128)S(1)} %get-tuple-element.427, pred[]{:T(512)S(6)} %compare.8, ...), kind=kOutput, calls=%fused_computation.2.clone.1.clone | convolution fusion | flops 545259520 | bytes 16908292 | tf_op jit(solution)/shard_map/while/body/eval_jaxpr/htk,kd->thd/dot_general | solution.py:77
  412.2 7.7 %constant_dynamic-slice_fusion.8 = f32[1,4,2048,256]{2,3,1,0:T(8,128)} fusion(f32[4,4,2048,256]{2,3,1,0:T(8,128)} %get-tuple-element.426, s32[]{:T(128)} %get-tuple-element.417), kind=kLoop, calls=%fused_computation.7.clone.1.clone | loop fusion | bytes 16777220 | tf_op jit(solution)/shard_map/while/body/jit(dynamic_index_in_dim)/dynamic_slice | solution.py:82
  419.8 8.7 %copy.53 = f32[1,4,2048,256]{3,2,1,0:T(8,128)} copy(f32[1,4,2048,256]{2,3,1,0:T(8,128)} %constant_dynamic-slice_fusion.8) | data formatting | bytes 16777216 | tf_op jit(solution)/shard_map/while/body/jit(dynamic_index_in_dim)/dynamic_slice | solution.py:82
  428.5 7.6 %bitcast_add_fusion.3 = f32[2048,4,128]{0,2,1:T(8,128)} fusion(f32[2048,4,128]{0,2,1:T(8,128)} %get-tuple-element.418, f32[4,2048]{1,0:T(4,128)S(1)} %get-tuple-element.428, f32[1,4,2048,256]{3,2,1,0:T(8,128)} %copy.53, f32[4,2048]{1,0:T(4,128)S(1)} %get-tuple-element.427, pred[]{:T(512)S(6)} %compare.8, ...), kind=kOutput, calls=%fused_computation.2.clone.1.clone | convolution fusion | flops 545259520 | bytes 16908292 | tf_op jit(solution)/shard_map/while/body/eval_jaxpr/htk,kd->thd/dot_general | solution.py:77
  440.2 41.3 %reduce-scatter.6.cloned.1.call-done = bf16[256,512]{0,1:T(8,128)(2,1)} async-done(((bf16[2048,512]{0,1:T(8,128)(2,1)}), bf16[256,512]{0,1:T(8,128)(2,1)}) %reduce-scatter.6.cloned.1.call-update) | async-done | bytes 262160 | tf_op jit(solution)/shard_map/reduce_scatter | solution.py:185
  481.6 5.7 fusion.25
  487.6 44.1 %all-gather.11.cloned.1.call-done = bf16[2048,512]{0,1:T(8,128)(2,1)} async-done(((bf16[256,512]{0,1:T(8,128)(2,1)}), bf16[2048,512]{0,1:T(8,128)(2,1)}) %all-gather.11.cloned.1.call-update) | async-done | bytes 2097168 | tf_op jit(solution)/shard_map/all_gather | solution.py:194
  532.3 6.0 convolution_convert_fusion
  538.3 81.9 %reduce-scatter.8.cloned.1.call-done = bf16[128,1024]{1,0:T(8,128)(2,1)} async-done(((bf16[2048,1024]{1,0:T(8,128)(2,1)}), bf16[128,1024]{1,0:T(8,128)(2,1)}) %reduce-scatter.8.cloned.1.call-update) | async-done | bytes 262160 | tf_op jit(solution)/shard_map/reduce_scatter | solution.py:196
  (87 shorter events, 42.1 us)
Async XLA Ops:
  6.5 27.4 %copy-start.1 = (bf16[1024,512]{1,0:T(8,128)(2,1)S(1)}, bf16[1024,512]{1,0:T(8,128)(2,1)}, u32[]{:S(2)}) copy-start(bf16[1024,512]{1,0:T(8,128)(2,1)} %param.18) | copy-start | bytes 3145732
  6.5 78.0 %all-gather.5.cloned.1.call-start = ((), (), s32[]{:S(2)}) async-start(), calls=%async_computation.3 | async-start | bytes 4456448 | tf_op jit(solution)/shard_map/all_gather | solution.py:106
  29.3 106.3 %reduce-scatter.4.cloned.1.call-start = ((), (), s32[]{:S(2)}) async-start(), calls=%async_computation.4 | async-start | bytes 3538944 | tf_op jit(solution)/shard_map/reduce_scatter | solution.py:128
  91.8 46.6 %copy-start.3 = (f32[512]{0:T(512)S(1)}, f32[512]{0:T(512)}, u32[]{:S(2)}) copy-start(f32[512]{0:T(512)} %param.20) | copy-start | bytes 6148
  91.8 83.2 %all-gather.9.cloned.1.call-start = ((), (), s32[]{:S(2)}) async-start(), calls=%async_computation.6 | async-start | bytes 1179648 | tf_op jit(solution)/shard_map/all_gather | solution.py:147
  137.9 85.7 %all-gather.7.cloned.1.call-start = ((), (), s32[]{:S(2)}) async-start(), calls=%async_computation.5 | async-start | bytes 2359296 | tf_op jit(solution)/shard_map/all_gather | solution.py:156
  140.2 341.3 %reduce-scatter.6.cloned.1.call-start = ((), (), s32[]{:S(2)}) async-start(), calls=%async_computation.7 | async-start | bytes 2359296 | tf_op jit(solution)/shard_map/reduce_scatter | solution.py:185
  177.6 3.2 copy-start
  436.2 45.4 %copy-start.2 = (bf16[2048,256]{0,1:T(8,128)(2,1)S(1)}, bf16[2048,256]{0,1:T(8,128)(2,1)}, u32[]{:S(2)}) copy-start(bf16[2048,256]{0,1:T(8,128)(2,1)} %all-gather.9.cloned.1.call-done) | copy-start | bytes 3145732
  440.1 91.5 %all-gather.11.cloned.1.call-start = ((), (), s32[]{:S(2)}) async-start(), calls=%async_computation.8 | async-start | bytes 2359296 | tf_op jit(solution)/shard_map/all_gather | solution.py:194
  481.6 50.1 %copy-start.4 = (f32[4,8]{1,0:T(4,128)S(1)}, f32[4,8]{1,0:T(4,128)}, u32[]{:S(2)}) copy-start(f32[4,8]{1,0:T(4,128)} %param.25) | copy-start | bytes 388
  481.6 50.7 %copy-start.5 = (bf16[512,1024]{1,0:T(8,128)(2,1)S(1)}, bf16[512,1024]{1,0:T(8,128)(2,1)}, u32[]{:S(2)}) copy-start(bf16[512,1024]{1,0:T(8,128)(2,1)} %param.24) | copy-start | bytes 3145732
  487.3 132.9 %reduce-scatter.8.cloned.1.call-start = ((), (), s32[]{:S(2)}) async-start(), calls=%async_computation.9 | async-start | bytes 4456448 | tf_op jit(solution)/shard_map/reduce_scatter | solution.py:196
Sparse Core Ops, SparseCore 0:
  29.5 55.0 all-gather.4
  91.9 43.6 reduce-scatter.3
  138.0 36.9 all-gather.8
  176.4 47.0 all-gather.6
  440.3 41.2 reduce-scatter.5
  487.4 44.1 all-gather.10
  538.4 81.7 reduce-scatter.7
where the time goes:
time: 628 us; the launch traced here: 627 us
  waiting for transfers between devices  332 us (53%)
  blocking collectives  83.6 us (13%)
  local copies, waits for them, and re-layouts  78.6 us (13%)
  matrix products  70.3 us (11%)
  other arithmetic  47 us (7%)
  between operations  14.4 us (2%)
    reduce_scatter x1, waiting for transfers between devices, body(): lax.psum_scatter(jnp.dot(attention_all, out_weight, preferred_element_typ...  81.9 us
    dynamic_slice x8, local copies, waits for them, and re-layouts, weighted_values(): return lax.scan(advance, start_state, (scores, value_blocks))[0]  65.5 us
    all_gather x1, waiting for transfers between devices, body(): gathered = lax.all_gather(normed, 'col', axis=0, tiled=True)  50.2 us
    all_gather x1, waiting for transfers between devices, body(): attention_all = lax.all_gather(attended, 'row', axis=0, tiled=True)  44.1 us
    reduce_scatter x1, waiting for transfers between devices, body(): lax.psum_scatter(jnp.dot(gathered, combined, preferred_element_type=jnp.f...  42.3 us
    reduce_scatter x1, waiting for transfers between devices, body(): lax.psum_scatter(cache_part.reshape(tokens, qwidth).astype(jnp.bfloat16),...  41.3 us
    all_gather x1, waiting for transfers between devices, body(): lax.all_gather(queries.reshape(tok_dev, qwidth), 'row', axis=0, tiled=True)  40.4 us
    dot_general x5, matrix products, advance(): jnp.einsum('htk,kd->thd', weights, block_item[1], preferred_element_type=...  35.5 us
  transfers between devices with their start and end apart: 7, of which 7 were waited for; matrix products, arithmetic and copies ran while one was open for 2% of the time, Pallas kernels for 0%

commit v1 on v0

v1 whole, which is shorter than its diff:
```python
import functools
import math

import jax
import jax.numpy as jnp
from jax import lax
from jax.experimental import pallas as pl
from jax.experimental.pallas import tpu as pltpu
from jax.sharding import Mesh
from jax.sharding import PartitionSpec as P

D = 8192
H = 64
KVH = 8
HD = 128
QB = 128
TOK = 128
GROUP = 8
SLOTS = 1024
HALF = 512

EPSILON = 1e-06
ROPE_BASE = 1000000.0
LOWEST = -1e30
ROW = ("ylo", "x")
COL = ("z", "yhi")
QSCALE = math.log2(math.e) / math.sqrt(HD)
PIECES = (0, 4, 1, 5, 3, 7, 2, 6)
VMEM = 48 * 2**20


def expand(block_scale):
    return jnp.repeat(jnp.repeat(block_scale, QB, axis=0), QB, axis=1)


def swap_cores(array):
    return lax.ppermute(array, "core", [(0, 1), (1, 0)])


def along(array, axis, size, distance):
    return lax.ppermute(array, axis, [(i, i ^ distance) for i in range(size)])


def gather(array, axes):
    return lax.all_to_all(
        jnp.broadcast_to(array[None], (GROUP,) + array.shape), axes, 0, 0, tiled=True
    )


def gather_cache(cache_keyval, head, core):
    mine = lax.dynamic_slice(cache_keyval, (0, core * HALF, head * HD), (2, HALF, HD))
    pair = jnp.stack([mine, along(mine, "ylo", 2, 1)])
    first = along(pair, "x", 4, 1)
    third = along(pair, "x", 4, 3)
    second_a = along(first[0:1], "x", 4, 3)
    second_b = along(third[1:2], "x", 4, 1)
    own = jnp.concatenate([pair, first, third, second_a, second_b], axis=0)
    return own, swap_cores(own)


def finish_kernel(parts_ref, ratio_ref, bias_ref, cos_ref, sin_ref, q_ref, kv_ref):
    ratio = ratio_ref[...]
    cosine = cos_ref[...]
    sine = sin_ref[...]
    for column in range(GROUP + 2):
        lanes = slice(column * HD, (column + 1) * HD)
        total = parts_ref[0, :, lanes].astype(jnp.float32)
        for part in range(1, GROUP):
            total = total + parts_ref[part, :, lanes].astype(jnp.float32)
        total = total * ratio + bias_ref[:, lanes]
        if column <= GROUP:
            total = total * cosine + pltpu.roll(total, HD // 2, 1) * sine
        if column < GROUP:
            q_ref[column] = (total * QSCALE).astype(jnp.bfloat16)
        else:
            kv_ref[column - GROUP] = total.astype(jnp.bfloat16)


def finish(parts, ratio, bias, cosine, sine):
    return pl.pallas_call(
        finish_kernel,
        out_shape=(
            jax.ShapeDtypeStruct((GROUP, TOK, HD), jnp.bfloat16),
            jax.ShapeDtypeStruct((2, TOK, HD), jnp.bfloat16),
        ),
        in_specs=[pl.BlockSpec(memory_space=pltpu.VMEM)] * 5,
        out_specs=(pl.BlockSpec(memory_space=pltpu.VMEM),) * 2,
        compiler_params=pltpu.CompilerParams(vmem_limit_bytes=VMEM),
    )(parts, ratio, bias, cosine, sine)


def with_ones(values):
    return jnp.concatenate([values, jnp.ones(values.shape, values.dtype)], axis=1)


def absorb(rows, query, keys, values, masks, peak_ref, acc_ref):
    scores = []
    for key, mask in zip(keys, masks, strict=True):
        score = lax.dot_general(
            query, key, (((1,), (1,)), ((), ())), preferred_element_type=jnp.float32
        )
        scores.append(score if mask is None else jnp.where(mask, score, LOWEST))
    old = peak_ref[rows, :]
    new = old
    for score in scores:
        new = jnp.maximum(new, jnp.max(score, axis=1, keepdims=True))
    fresh = None
    for score, value in zip(scores, values, strict=True):
        weights = jnp.exp2(score - new).astype(jnp.bfloat16)
        part = jnp.dot(weights, value, preferred_element_type=jnp.float32)
        fresh = part if fresh is None else fresh + part
    acc_ref[rows, :] = acc_ref[rows, :] * jnp.exp2(old - new) + fresh
    peak_ref[rows, :] = new


CHUNK = 256
ROWS = GROUP * TOK


def cache_kernel(place_ref, q_ref, own_ref, peer_ref, acc_ref, peak_ref):
    offset = place_ref[0]
    core = place_ref[1]
    acc_ref[...] = jnp.zeros_like(acc_ref)
    peak_ref[...] = jnp.full_like(peak_ref, LOWEST)

    def piece(index, carry):
        base = place_ref[2 + index] * SLOTS
        own_base = base + core * HALF
        peer_base = base + (1 - core) * HALF

        def step(masked):
            keys = [own_ref[index, 0], peer_ref[index, 0]]
            values = [with_ones(own_ref[index, 1]), with_ones(peer_ref[index, 1])]
            masks = [None, None]
            if masked:
                slot = lax.broadcasted_iota(jnp.int32, (CHUNK, HALF), 1)
                masks = [slot + own_base < offset, slot + peer_base < offset]
            for start in range(0, ROWS, CHUNK):
                rows = slice(start, start + CHUNK)
                absorb(rows, q_ref[rows, :], keys, values, masks, peak_ref, acc_ref)

        @pl.when(base + SLOTS <= offset)
        def _():
            step(False)

        @pl.when((base < offset) & (base + SLOTS > offset))
        def _():
            step(True)

        return carry

    lax.fori_loop(0, GROUP, piece, 0)


def attend_cache(place, queries, own, peer):
    return pl.pallas_call(
        cache_kernel,
        out_shape=(
            jax.ShapeDtypeStruct((ROWS, 2 * HD), jnp.float32),
            jax.ShapeDtypeStruct((ROWS, 1), jnp.float32),
        ),
        in_specs=[pl.BlockSpec(memory_space=pltpu.SMEM)]
        + [pl.BlockSpec(memory_space=pltpu.VMEM)] * 3,
        out_specs=(pl.BlockSpec(memory_space=pltpu.VMEM),) * 2,
        compiler_params=pltpu.CompilerParams(vmem_limit_bytes=VMEM),
        cost_estimate=pl.CostEstimate(
            flops=16 * 2**30, bytes_accessed=8 * 2**20, transcendentals=2**23
        ),
    )(place, queries, own, peer)


def span_kernel(place_ref, q_ref, own_ref, peer_ref, acc_in, peak_in, out_ref, acc_ref, peak_ref):
    core = place_ref[1]
    mine = 2 * place_ref[2] + core
    acc_ref[...] = acc_in[...]
    peak_ref[...] = peak_in[...]
    blocks = 4
    width = blocks * TOK
    for start in range(0, GROUP, blocks):
        for ref, other in ((own_ref, core), (peer_ref, 1 - core)):
            first = 2 * start + other
            last = first + 2 * (blocks - 1)

            def step(masked, ref=ref, start=start, first=first):
                key = ref[start : start + blocks, 0].reshape(width, HD)
                value = with_ones(ref[start : start + blocks, 1].reshape(width, HD))
                mask = None
                if masked:
                    lane = lax.broadcasted_iota(jnp.int32, (CHUNK, width), 1)
                    token = (first + 2 * (lane // TOK)) * TOK + lane % TOK
                    row = lax.broadcasted_iota(jnp.int32, (CHUNK, width), 0)
                    mask = token <= mine * TOK + row % TOK
                for begin in range(0, ROWS, CHUNK):
                    rows = slice(begin, begin + CHUNK)
                    absorb(rows, q_ref[rows, :], [key], [value], [mask], peak_ref, acc_ref)

            @pl.when(last < mine)
            def _(step=step):
                step(False)

            @pl.when((first <= mine) & (last >= mine))
            def _(step=step):
                step(True)

    for head in range(GROUP):
        rows = slice(head * TOK, (head + 1) * TOK)
        out_ref[:, head * HD : (head + 1) * HD] = (
            acc_ref[rows, :HD] / acc_ref[rows, HD:]
        ).astype(jnp.bfloat16)


def attend_span(place, queries, own, peer, acc, peak):
    return pl.pallas_call(
        span_kernel,
        out_shape=jax.ShapeDtypeStruct((TOK, GROUP * HD), jnp.bfloat16),
        in_specs=[pl.BlockSpec(memory_space=pltpu.SMEM)]
        + [pl.BlockSpec(memory_space=pltpu.VMEM)] * 5,
        out_specs=pl.BlockSpec(memory_space=pltpu.VMEM),
        scratch_shapes=[
            pltpu.VMEM((ROWS, 2 * HD), jnp.float32),
            pltpu.VMEM((ROWS, 1), jnp.float32),
        ],
        compiler_params=pltpu.CompilerParams(vmem_limit_bytes=VMEM),
        cost_estimate=pl.CostEstimate(
            flops=4 * 2**30, bytes_accessed=4 * 2**20, transcendentals=2**21
        ),
    )(place, queries, own, peer, acc, peak)


def body(
    hidden_in,
    norm_gain,
    w_query,
    scale_query,
    bias_query,
    w_keyval,
    scale_keyval,
    bias_keyval,
    w_out,
    scale_out,
    cache_keyval,
    span_offset,
):
    row = lax.axis_index(ROW)
    head = lax.axis_index(COL)
    core = lax.axis_index("core")
    offset = span_offset[0]

    gathered = gather(hidden_in, COL).reshape(GROUP * TOK, -1)

    widened = hidden_in.astype(jnp.float32)
    squares = lax.psum(jnp.sum(widened * widened, axis=1), ROW)
    ratio = lax.ppermute(
        lax.rsqrt(squares / D + EPSILON),
        ROW + COL,
        [(r * GROUP + b, b * GROUP + r) for r in range(GROUP) for b in range(GROUP)],
    )

    query_own = (
        w_query.astype(jnp.float32) * expand(scale_query) * norm_gain[:, None]
    ).astype(jnp.bfloat16)
    query_peer = swap_cores(query_own)
    bias_peer = swap_cores(bias_query)
    keyval = []
    bias = [bias_query, bias_peer]
    for kind in range(2):
        start = kind * KVH + head
        weight = lax.dynamic_slice_in_dim(w_keyval, start * HD, HD, 1)
        scale = lax.dynamic_slice_in_dim(scale_keyval, start, 1, 1)
        keyval.append(
            (weight.astype(jnp.float32) * expand(scale) * norm_gain[:, None]).astype(jnp.bfloat16)
        )
        bias.append(lax.dynamic_slice_in_dim(bias_keyval, start * HD, HD, 0))
    weights = jnp.concatenate([query_own, query_peer] + keyval, axis=1)
    bias = jnp.concatenate(bias)[None, :]

    out_own = (w_out.astype(jnp.float32) * expand(scale_out)).astype(jnp.bfloat16)
    out_weight = jnp.concatenate([out_own, swap_cores(out_own)], axis=0)

    cache_own, cache_peer = gather_cache(cache_keyval, head, core)

    token = (2 * row + core) * TOK + jnp.arange(TOK, dtype=jnp.int32)
    positions = (offset + token).astype(jnp.float32)
    inverse = ROPE_BASE ** (-(2.0 * jnp.arange(HD // 2, dtype=jnp.float32)) / HD)
    angles = positions[:, None] * inverse[None, :]
    cosine = jnp.cos(angles)
    sine = jnp.sin(angles)
    cosine = jnp.concatenate([cosine, cosine], axis=1)
    sine = jnp.concatenate([-sine, sine], axis=1)

    projected = jnp.dot(gathered, weights, preferred_element_type=jnp.float32).astype(jnp.bfloat16)
    parts = lax.all_to_all(projected.reshape(GROUP, TOK, -1), ROW, 0, 0, tiled=True)
    queries, own_kv = finish(parts, ratio[:, None], bias, cosine, sine)
    queries = queries.reshape(ROWS, HD)

    span_own = gather(own_kv, ROW)
    span_peer = swap_cores(span_own)

    order = jnp.array(PIECES, jnp.int32) ^ row
    place = jnp.concatenate([jnp.stack([offset, core]), order]).astype(jnp.int32)
    acc, peak = attend_cache(place, queries, cache_own, cache_peer)
    attended = attend_span(place, queries, span_own, span_peer, acc, peak)

    everyone = gather(attended, ROW).reshape(GROUP * TOK, -1)
    mixed = jnp.dot(everyone, out_weight, preferred_element_type=jnp.float32).astype(jnp.bfloat16)
    shares = lax.all_to_all(mixed.reshape(GROUP, TOK, -1), COL, 0, 0, tiled=True)
    return jnp.sum(shares.astype(jnp.float32), axis=0).astype(jnp.bfloat16)


def solution(mesh):
    fine = Mesh(mesh.devices.reshape(2, 4, 4, 2, 2), ("ylo", "x", "z", "yhi", "core"))
    row = ("ylo", "x")
    col = ("z", "yhi", "core")
    return jax.shard_map(
        body,
        mesh=fine,
        in_specs=(
            P(col, row),
            P(row),
            P(row, col),
            P(row, col),
            P(col),
            P(row, None),
            P(row, None),
            P(),
            P(col, row),
            P(col, row),
            P(None, row, None),
            P(),
        ),
        out_specs=P(col, row),
        check_vma=False,
    )
```

time: 628 us -> 240 us (0.38)
  waiting for transfers between devices: 332 us -> 94.1 us
  matrix products: 70.3 us -> 9.47 us
  local copies, waits for them, and re-layouts: 78.6 us -> 19.7 us
  other arithmetic: 47 us -> 6.1 us
  starting transfers between devices: 0.65 us -> 38.7 us
  blocking collectives: 83.6 us -> 52.2 us
  Pallas kernels: 0 us -> 16 us
  between operations: 14.4 us -> 0.92 us
    all_gather x4 -> x0, waiting for transfers between devices: 167 us -> none  [the longest x1 50.2 us: body(): gathered = lax.all_gather(normed, 'col', axis=0, tiled=True)]
    reduce_scatter x3 -> x0, waiting for transfers between devices: 166 us -> none  [the longest x1 81.9 us: body(): lax.psum_scatter(jnp.dot(attention_all, out_weight, preferred_element_typ...]
    dynamic_slice x11 -> x2, local copies, waits for them, and re-layouts: 67.2 us -> 1 us  [the longest x1 0.78 us: body(): bias.append(lax.dynamic_slice_in_dim(bias_keyval, start * HD, HD, 0))]
    dot_general x12 -> x2, matrix products: 70.3 us -> 9.47 us  [the longest x1 5.92 us: body(): jnp.dot(gathered, weights, preferred_element_type=jnp.float32)]
    ppermute x0 -> x11, waiting for transfers between devices: none -> 60.7 us  [the longest x5 58.1 us: along(): return lax.ppermute(array, axis, [(i, i ^ distance) for i in range(size)])]
    all_to_all x0 -> x4, waiting for transfers between devices: none -> 33.4 us  [the longest x3 33.4 us: gather(): lax.all_to_all(jnp.broadcast_to(array[None], (GROUP,) + array.shape), axe...]
    pmax x1 -> x0, blocking collectives: 33.2 us -> none  [body(): lax.pmax(jnp.maximum(cache_peak, placed_peak).astype(jnp.bfloat16), 'row')]
    all_to_all x0 -> x1, blocking collectives: none -> 33.2 us  [body(): lax.all_to_all(mixed.reshape(GROUP, TOK, -1), COL, 0, 0, tiled=True)]
  transfers between devices with their start and end apart: 7 -> 15, of which waited for: 7 -> 6; matrix products, arithmetic and copies ran while one was open for 2% -> 10% of each run, Pallas kernels for 0% -> 6%
where the time goes in v1:
time: 240 us; the launch traced here: 237 us
  waiting for transfers between devices  94.1 us (39%)
  blocking collectives  52.2 us (22%)
  starting transfers between devices  38.7 us (16%)
  local copies, waits for them, and re-layouts  19.7 us (8%)
  Pallas kernels  16 us (7%)
  matrix products  9.47 us (4%)
  other arithmetic  6.1 us (3%)
    ppermute x5, waiting for transfers between devices, along(): return lax.ppermute(array, axis, [(i, i ^ distance) for i in range(size)])  58.1 us
    all_to_all x3, waiting for transfers between devices, gather(): lax.all_to_all(jnp.broadcast_to(array[None], (GROUP,) + array.shape), axe...  33.4 us
    all_to_all x1, blocking collectives, body(): lax.all_to_all(mixed.reshape(GROUP, TOK, -1), COL, 0, 0, tiled=True)  33.2 us
    all_to_all x3, starting transfers between devices, gather(): lax.all_to_all(jnp.broadcast_to(array[None], (GROUP,) + array.shape), axe...  24.9 us
    psum x1, blocking collectives, body(): squares = lax.psum(jnp.sum(widened * widened, axis=1), ROW)  19 us
    pallas_call x1, Pallas kernels, attend_cache(): pl.pallas_call(cache_kernel, out_shape=(jax.ShapeDtypeStruct((ROWS, 2 * H...  13.2 us
    unnamed x26, local copies, waits for them, and re-layouts  9.13 us
    ppermute x5, starting transfers between devices, along(): return lax.ppermute(array, axis, [(i, i ^ distance) for i in range(size)])  9.09 us
  transfers between devices with their start and end apart: 15, of which 6 were waited for; matrix products, arithmetic and copies ran while one was open for 10% of the time, Pallas kernels for 6%

profile of v1, /device:TPU:0, one launch (start us, length us, event | category | flops | bytes accessed | tf_op | source)
XLA Modules:
  0.0 237.2 jit_solution(12013547682822584305)
XLA Ops:
  0.0 2.5 %broadcast_in_dim.59 = bf16[8,128,1024]{2,1,0:T(8,128)(2,1)} broadcast(bf16[128,1024]{1,0:T(8,128)(2,1)} %param.13), dimensions={1,2} | broadcast | bytes 2359296 | tf_op jit(solution)/shard_map/broadcast_in_dim | solution.py:46
  2.5 8.2 %all-to-all-start = ((bf16[8,128,1024]{2,1,0:T(8,128)(2,1)}), bf16[8,128,1024]{2,1,0:T(8,128)(2,1)S(1)}, u32[]{:S(2)}, u32[]{:S(2)}) async-start(bf16[8,128,1024]{2,1,0:T(8,128)(2,1)} %broadcast_in_dim.59), calls=%async_computation | async-start | bytes 4194304 | tf_op jit(solution)/shard_map/all_to_all | solution.py:45
  10.9 1.2 broadcast_in_dim.54
  12.1 1.3 fusion.9
  13.4 1.7 constant_dynamic-update-slice_fusion.5
  15.8 24.4 %collective-permute-done.4 = bf16[2,512,128]{2,1,0:T(8,128)(2,1)S(1)} collective-permute-done((bf16[2,512,128]{2,1,0:T(8,128)(2,1)S(1)}, bf16[2,512,128]{2,1,0:T(8,128)(2,1)S(1)}, u32[]{:S(2)}, u32[]{:S(2)}) %collective-permute-start.4) | collective-permute-done | bytes 262176 | tf_op jit(solution)/shard_map/ppermute | solution.py:41
  41.0 1.5 collective-permute-start.5
  42.8 1.5 multiply_convert_fusion.1
  44.3 2.2 collective-permute-start.6
  46.5 7.5 %collective-permute-done.5 = bf16[2,2,512,128]{3,2,1,0:T(8,128)(2,1)S(1)} collective-permute-done((bf16[2,2,512,128]{3,2,1,0:T(8,128)(2,1)}, bf16[2,2,512,128]{3,2,1,0:T(8,128)(2,1)S(1)}, u32[]{:S(2)}, u32[]{:S(2)}) %collective-permute-start.5) | collective-permute-done | bytes 524320 | tf_op jit(solution)/shard_map/ppermute | solution.py:41
  54.7 2.8 %collective-permute-start.7 = (bf16[1,2,512,128]{3,2,1,0:T(8,128)(2,1)}, bf16[1,2,512,128]{3,2,1,0:T(8,128)(2,1)}, u32[]{:S(2)}, u32[]{:S(2)}) collective-permute-start(bf16[1,2,512,128]{3,2,1,0:T(8,128)(2,1)} %slice.8), channel_id=1, source_target_pairs={{0,48},{16,32},{32,16},{48,0},{1,49},{17,33},{33,17},{49,1},{2,50}... | collective-permute-start | bytes 786440 | tf_op jit(solution)/shard_map/ppermute | solution.py:41
  57.5 5.9 %convolution_convert_fusion = bf16[1280,1024]{0,1:T(8,128)(2,1)} fusion(bf16[1024,1024]{1,0:T(8,128)(2,1)S(1)} %bitcast.41, bf16[1024,128]{1,0:T(8,128)(2,1)S(1)} %get-tuple-element.18, bf16[1024,128]{1,0:T(8,128)(2,1)S(1)} %get-tuple-element.17, bf16[1024,512]{1,0:T(8,128)(2,1)} %collective-permute-done, bf16[1024,512]{1,0:T(8,128)(2,1)} %fusion.9), kind=kOutput, calls=%fused_computation | convolution fusion | flops 2696151040 | bytes 7340032 | tf_op jit(solution)/shard_map/dot_general | solution.py:291
  63.4 3.6 %all-to-all-start.1 = ((bf16[8,128,1280]{2,1,0:T(8,128)(2,1)}), bf16[8,128,1280]{2,1,0:T(8,128)(2,1)S(1)}, u32[]{:S(2)}, u32[]{:S(2)}) async-start(bf16[8,128,1280]{2,1,0:T(8,128)(2,1)} %bitcast.39), calls=%async_computation.1 | async-start | bytes 5242880 | tf_op jit(solution)/shard_map/all_to_all | solution.py:292
  67.8 1.0 slice.9
  68.8 2.0 collective-permute-start.8
  71.6 1.9 constant_dynamic-update-slice_fusion.2
  73.4 1.7 constant_dynamic-update-slice_fusion.1
  75.1 26.2 %collective-permute-done.8 = bf16[1,2,512,128]{3,2,1,0:T(8,128)(2,1)S(1)} collective-permute-done((bf16[1,2,512,128]{3,2,1,0:T(8,128)(2,1)S(1)}, bf16[1,2,512,128]{3,2,1,0:T(8,128)(2,1)S(1)}, u32[]{:S(2)}, u32[]{:S(2)}) %collective-permute-start.8) | collective-permute-done | bytes 262176 | tf_op jit(solution)/shard_map/ppermute | solution.py:41
  102.2 19.0 %psum.7 = f32[128]{0:T(128)S(1)} all-reduce(f32[128]{0:T(128)S(1)} %multiply_reduce_fusion), channel_id=1, replica_groups=mesh['ylo'=2,'x'=4,'z'=4,'yhi'=2,'core'=2] {'ylo','x'}, use_global_device_ids=true, to_apply=%region_1.0 | all-reduce | flops 128 | bytes 1024 | tf_op jit(solution)/shard_map/psum | solution.py:252
  124.5 0.9 broadcast_in_dim.62
  125.4 9.8 %all-to-all-start.2 = ((bf16[8,2,128,128]{3,2,1,0:T(8,128)(2,1)}), bf16[8,2,128,128]{3,2,1,0:T(8,128)(2,1)S(1)}, u32[]{:S(2)}, u32[]{:S(2)}) async-start(bf16[8,2,128,128]{3,2,1,0:T(8,128)(2,1)} %broadcast_in_dim.62), calls=%async_computation.2 | async-start | bytes 1048576 | tf_op jit(solution)/shard_map/all_to_all | solution.py:45
  135.3 10.7 %all-to-all-done.2.own_ref = bf16[8,2,128,128]{3,2,1,0:T(8,128)(2,1)S(1)} async-done(((bf16[8,2,128,128]{3,2,1,0:T(8,128)(2,1)}), bf16[8,2,128,128]{3,2,1,0:T(8,128)(2,1)S(1)}, u32[]{:S(2)}, u32[]{:S(2)}) %all-to-all-start.2) | async-done | bytes 524320 | tf_op jit(solution)/shard_map/all_to_all | solution.py:45
  146.0 1.6 copy-done
  147.6 13.2 %shard_map.128 = (f32[1024,256]{1,0:T(8,128)S(1)}, f32[1024,1]{1,0:T(8,128)S(1)}) custom-call(s32[10]{0:T(128)S(1)} %pad_add_fusion.place_ref, bf16[1024,128]{1,0:T(8,128)(2,1)S(1)} %bitcast.35, bf16[8,2,512,128]{3,2,1,0:T(8,128)(2,1)S(1)} %copy-done, bf16[8,2,512,128]{3,2,1,0:T(8,128)(2,1)} %collective-permute-done.9.peer_ref), custom_call_target="tpu_custom_call" | custom-call | flops 17179869184 | bytes 8388608 | tf_op jit(solution)/shard_map/pallas_call | solution.py:156
  160.8 2.3 shard_map.129
  163.2 1.6 broadcast_in_dim.63
  164.8 7.0 %all-to-all-start.3 = ((bf16[8,128,1024]{2,1,0:T(8,128)(2,1)}), bf16[8,128,1024]{2,1,0:T(8,128)(2,1)S(1)}, u32[]{:S(2)}, u32[]{:S(2)}) async-start(bf16[8,128,1024]{2,1,0:T(8,128)(2,1)} %broadcast_in_dim.63), calls=%async_computation.3 | async-start | bytes 4194304 | tf_op jit(solution)/shard_map/all_to_all | solution.py:45
  174.0 2.6 %collective-permute-done.10 = bf16[512,1024]{1,0:T(8,128)(2,1)} collective-permute-done((bf16[512,1024]{1,0:T(8,128)(2,1)S(1)}, bf16[512,1024]{1,0:T(8,128)(2,1)}, u32[]{:S(2)}, u32[]{:S(2)}) %collective-permute-start.10) | collective-permute-done | bytes 1048608 | tf_op jit(solution)/shard_map/ppermute | solution.py:37
  176.6 22.8 %all-to-all-done.3 = bf16[8,128,1024]{2,1,0:T(8,128)(2,1)S(1)} async-done(((bf16[8,128,1024]{2,1,0:T(8,128)(2,1)}), bf16[8,128,1024]{2,1,0:T(8,128)(2,1)S(1)}, u32[]{:S(2)}, u32[]{:S(2)}) %all-to-all-start.3) | async-done | bytes 2097184 | tf_op jit(solution)/shard_map/all_to_all | solution.py:45
  199.3 3.6 %fusion.14 = bf16[1024,1024]{1,0:T(8,128)(2,1)S(1)} fusion(bf16[1024,1024]{1,0:T(8,128)(2,1)S(1)} %bitcast.42, bf16[512,1024]{1,0:T(8,128)(2,1)} %collective-permute-done.10, bf16[512,1024]{1,0:T(8,128)(2,1)S(1)} %fusion.7), kind=kOutput, calls=%fused_computation.17 | convolution fusion | flops 2152726528 | bytes 6291456 | tf_op jit(solution)/shard_map/dot_general | solution.py:305
  202.9 33.2 %all_to_all.25 = bf16[8,128,1024]{2,1,0:T(8,128)(2,1)S(1)} all-to-all(bf16[8,128,1024]{2,1,0:T(8,128)(2,1)S(1)} %bitcast.43), channel_id=1, replica_groups=mesh['ylo'=2,'x'=4,'z'=4,'yhi'=2,'core'=2] {'z','yhi'}, dimensions={0} | all-to-all | bytes 4194304 | tf_op jit(solution)/shard_map/all_to_all | solution.py:306
  236.1 1.1 reduce_sum.22
  (60 shorter events, 10.0 us)
Async XLA Ops:
  2.5 8.2 %copy-start.7 = (f32[8,4]{0,1:T(4,128)S(1)}, f32[8,4]{0,1:T(4,128)}, u32[]{:S(2)}) copy-start(f32[8,4]{0,1:T(4,128)} %param.16) | copy-start | bytes 388
  2.5 55.0 %all-to-all-start = ((bf16[8,128,1024]{2,1,0:T(8,128)(2,1)}), bf16[8,128,1024]{2,1,0:T(8,128)(2,1)S(1)}, u32[]{:S(2)}, u32[]{:S(2)}) async-start(bf16[8,128,1024]{2,1,0:T(8,128)(2,1)} %broadcast_in_dim.59), calls=%async_computation | async-start | bytes 4194304 | tf_op jit(solution)/shard_map/all_to_all | solution.py:45
  10.7 1.4 copy-start.1
  10.7 1.4 copy-start.4
  12.1 30.4 %copy-start.5 = (f32[8,16]{1,0:T(8,128)S(1)}, f32[8,16]{1,0:T(8,128)}, u32[]{:S(2)}) copy-start(f32[8,16]{1,0:T(8,128)} %param.19) | copy-start | bytes 1540
  13.4 44.1 %collective-permute-start = (bf16[1024,512]{1,0:T(8,128)(2,1)}, bf16[1024,512]{1,0:T(8,128)(2,1)}, u32[]{:S(2)}, u32[]{:S(2)}) collective-permute-start(bf16[1024,512]{1,0:T(8,128)(2,1)} %fusion.9), channel_id=1, source_target_pairs={{0,1},{1,0},{2,3},{3,2},{4,5},{5,4},{6,7},{7,6},{8,9},{9,8},{10,11... | collective-permute-start | bytes 3145736 | tf_op jit(solution)/shard_map/ppermute | solution.py:37
  15.1 25.0 %collective-permute-start.4 = (bf16[2,512,128]{2,1,0:T(8,128)(2,1)S(1)}, bf16[2,512,128]{2,1,0:T(8,128)(2,1)S(1)}, u32[]{:S(2)}, u32[]{:S(2)}) collective-permute-start(bf16[2,512,128]{2,1,0:T(8,128)(2,1)S(1)} %get-tuple-element.16), channel_id=1, source_target_pairs={{0,64},{64,0},{1,65},{65,1},{2,66},{66,2},{3,67},{67,3},{4,68},{68... | collective-permute-start | bytes 786440 | tf_op jit(solution)/shard_map/ppermute | solution.py:41
  41.0 13.0 %collective-permute-start.5 = (bf16[2,2,512,128]{3,2,1,0:T(8,128)(2,1)}, bf16[2,2,512,128]{3,2,1,0:T(8,128)(2,1)S(1)}, u32[]{:S(2)}, u32[]{:S(2)}) collective-permute-start(bf16[2,2,512,128]{3,2,1,0:T(8,128)(2,1)} %pad_maximum_fusion), channel_id=1, source_target_pairs={{0,16},{16,0},{32,48},{48,32},{1,17},{17,1},{33,49},{49,33},{2,18}... | collective-permute-start | bytes 1572872 | tf_op jit(solution)/shard_map/ppermute | solution.py:41
  44.3 23.5 %collective-permute-start.6 = (bf16[2,2,512,128]{3,2,1,0:T(8,128)(2,1)}, bf16[2,2,512,128]{3,2,1,0:T(8,128)(2,1)}, u32[]{:S(2)}, u32[]{:S(2)}) collective-permute-start(bf16[2,2,512,128]{3,2,1,0:T(8,128)(2,1)} %pad_maximum_fusion), channel_id=1, source_target_pairs={{0,48},{16,32},{32,16},{48,0},{1,49},{17,33},{33,17},{49,1},{2,50}... | collective-permute-start | bytes 1572872 | tf_op jit(solution)/shard_map/ppermute | solution.py:41
  54.7 18.7 %collective-permute-start.7 = (bf16[1,2,512,128]{3,2,1,0:T(8,128)(2,1)}, bf16[1,2,512,128]{3,2,1,0:T(8,128)(2,1)}, u32[]{:S(2)}, u32[]{:S(2)}) collective-permute-start(bf16[1,2,512,128]{3,2,1,0:T(8,128)(2,1)} %slice.8), channel_id=1, source_target_pairs={{0,48},{16,32},{32,16},{48,0},{1,49},{17,33},{33,17},{49,1},{2,50}... | collective-permute-start | bytes 786440 | tf_op jit(solution)/shard_map/ppermute | solution.py:41
  63.4 60.6 %all-to-all-start.1 = ((bf16[8,128,1280]{2,1,0:T(8,128)(2,1)}), bf16[8,128,1280]{2,1,0:T(8,128)(2,1)S(1)}, u32[]{:S(2)}, u32[]{:S(2)}) async-start(bf16[8,128,1280]{2,1,0:T(8,128)(2,1)} %bitcast.39), calls=%async_computation.1 | async-start | bytes 5242880 | tf_op jit(solution)/shard_map/all_to_all | solution.py:292
  67.1 35.0 %copy-start.2 = (bf16[128,1024]{1,0:T(8,128)(2,1)S(1)}, bf16[128,1024]{1,0:T(8,128)(2,1)}, u32[]{:S(2)}) copy-start(bf16[128,1024]{1,0:T(8,128)(2,1)} %param.13) | copy-start | bytes 786436
  67.8 54.1 %copy-start.8 = (f32[512]{0:T(512)S(1)}, f32[512]{0:T(512)}, u32[]{:S(2)}) copy-start(f32[512]{0:T(512)} %param.17) | copy-start | bytes 6148
  68.8 32.5 %collective-permute-start.8 = (bf16[1,2,512,128]{3,2,1,0:T(8,128)(2,1)S(1)}, bf16[1,2,512,128]{3,2,1,0:T(8,128)(2,1)S(1)}, u32[]{:S(2)}, u32[]{:S(2)}) collective-permute-start(bf16[1,2,512,128]{3,2,1,0:T(8,128)(2,1)S(1)} %slice.9), channel_id=1, source_target_pairs={{0,16},{16,0},{32,48},{48,32},{1,17},{17,1},{33,49},{49,33},{2,18}... | collective-permute-start | bytes 786440 | tf_op jit(solution)/shard_map/ppermute | solution.py:41
  102.1 43.9 %collective-permute-start.9 = (bf16[8,2,512,128]{3,2,1,0:T(8,128)(2,1)}, bf16[8,2,512,128]{3,2,1,0:T(8,128)(2,1)}, u32[]{:S(2)}, u32[]{:S(2)}) collective-permute-start(bf16[8,2,512,128]{3,2,1,0:T(8,128)(2,1)} %constant_dynamic-update-slice_fusion.own_ref), channel_id=1, source_target_pairs={{0,1},{1,0},{2,3},{3,2},{4,5},{5,4},{6,7},{7,6},{8,9},{9,8},{10,11... | collective-permute-start | bytes 6291464 | tf_op jit(solution)/shard_map/ppermute | solution.py:37
  121.2 2.7 %collective-permute-start.1 = (f32[128]{0:T(128)S(1)}, f32[128]{0:T(128)S(1)}, u32[]{:S(2)}, u32[]{:S(2)}) collective-permute-start(f32[128]{0:T(128)S(1)} %add_rsqrt_fusion), channel_id=1, source_target_pairs={{0,0},{2,16},{4,32},{6,48},{8,64},{10,80},{12,96},{14,112},{16,2},... | collective-permute-start | bytes 1544 | tf_op jit(solution)/shard_map/ppermute | solution.py:253
  121.9 2.1 collective-permute-start.2
  124.0 11.2 %copy-start.9 = (s32[8]{0:T(128)S(1)}, s32[8]{0:T(128)}, u32[]{:S(2)}) copy-start(s32[8]{0:T(128)} %constant.57.clone) | copy-start | bytes 100
  125.4 20.6 %all-to-all-start.2 = ((bf16[8,2,128,128]{3,2,1,0:T(8,128)(2,1)}), bf16[8,2,128,128]{3,2,1,0:T(8,128)(2,1)S(1)}, u32[]{:S(2)}, u32[]{:S(2)}) async-start(bf16[8,2,128,128]{3,2,1,0:T(8,128)(2,1)} %broadcast_in_dim.62), calls=%async_computation.2 | async-start | bytes 1048576 | tf_op jit(solution)/shard_map/all_to_all | solution.py:45
  146.0 14.8 %collective-permute-start.3 = (bf16[8,2,128,128]{3,2,1,0:T(8,128)(2,1)S(1)}, bf16[8,2,128,128]{3,2,1,0:T(8,128)(2,1)S(1)}, u32[]{:S(2)}, u32[]{:S(2)}) collective-permute-start(bf16[8,2,128,128]{3,2,1,0:T(8,128)(2,1)S(1)} %all-to-all-done.2.own_ref), channel_id=1, source_target_pairs={{0,1},{1,0},{2,3},{3,2},{4,5},{5,4},{6,7},{7,6},{8,9},{9,8},{10,11... | collective-permute-start | bytes 1572872 | tf_op jit(solution)/shard_map/ppermute | solution.py:37
  146.0 1.6 copy-start
  164.8 7.0 %copy-start.6 = (f32[4,8]{1,0:T(4,128)S(1)}, f32[4,8]{1,0:T(4,128)}, u32[]{:S(2)}) copy-start(f32[4,8]{1,0:T(4,128)} %param.22) | copy-start | bytes 388
  164.8 34.5 %all-to-all-start.3 = ((bf16[8,128,1024]{2,1,0:T(8,128)(2,1)}), bf16[8,128,1024]{2,1,0:T(8,128)(2,1)S(1)}, u32[]{:S(2)}, u32[]{:S(2)}) async-start(bf16[8,128,1024]{2,1,0:T(8,128)(2,1)} %broadcast_in_dim.63), calls=%async_computation.3 | async-start | bytes 4194304 | tf_op jit(solution)/shard_map/all_to_all | solution.py:45
  171.7 1.2 copy-start.3
  173.7 2.9 %collective-permute-start.10 = (bf16[512,1024]{1,0:T(8,128)(2,1)S(1)}, bf16[512,1024]{1,0:T(8,128)(2,1)}, u32[]{:S(2)}, u32[]{:S(2)}) collective-permute-start(bf16[512,1024]{1,0:T(8,128)(2,1)S(1)} %fusion.7), channel_id=1, source_target_pairs={{0,1},{1,0},{2,3},{3,2},{4,5},{5,4},{6,7},{7,6},{8,9},{9,8},{10,11... | collective-permute-start | bytes 3145736 | tf_op jit(solution)/shard_map/ppermute | solution.py:37

commit v2 on v1

v2 whole, which is shorter than its diff:
```python
import functools
import math

import jax
import jax.numpy as jnp
from jax import lax
from jax.experimental import pallas as pl
from jax.experimental.pallas import tpu as pltpu
from jax.sharding import Mesh
from jax.sharding import PartitionSpec as P

D = 8192
H = 64
KVH = 8
HD = 128
QB = 128
TOK = 128
GROUP = 8
SLOTS = 1024
HALF = 512

EPSILON = 1e-06
ROPE_BASE = 1000000.0
LOWEST = -1e30
ROW = ("ylo", "x")
COL = ("z", "yhi")
QSCALE = math.log2(math.e) / math.sqrt(HD)
WIDE = 640
SQUARES = 2 * WIDE
PART = 64
NEAR = (0, 4, 3, 7)
FAR = (1, 5, 2, 6)
MEMBERS = ((0, 3, 4, 7), (1, 2, 5, 6))
VMEM = 48 * 2**20


def expand(block_scale):
    return jnp.repeat(jnp.repeat(block_scale, QB, axis=0), QB, axis=1)


def swap_cores(array):
    return lax.ppermute(array, "core", [(0, 1), (1, 0)])


def along(array, axis, size, distance):
    return lax.ppermute(array, axis, [(i, i ^ distance) for i in range(size)])


def beside(array):
    return along(array, "x", 4, 1)


def exchange(array, axes, groups=None):
    return lax.all_to_all(array, axes, 0, 0, tiled=True, axis_index_groups=groups)


def copies(array, count):
    return jnp.broadcast_to(array[None], (count,) + array.shape)


def in_vmem(count):
    return [pl.BlockSpec(memory_space=pltpu.VMEM)] * count


def place_of(block):
    return (block, 0) if block < 4 else (7 - block, PART)


def project_kernel(x_ref, own_ref, own_x_ref, peer_ref, peer_x_ref, out_ref):
    rows = GROUP * PART
    x = x_ref[...].reshape(rows, 2 * SLOTS)
    for start, near, far in ((0, own_ref, own_x_ref), (WIDE, peer_ref, peer_x_ref)):
        total = jnp.dot(x[:, :SLOTS], near[...], preferred_element_type=jnp.float32)
        total = total + jnp.dot(x[:, SLOTS:], far[...], preferred_element_type=jnp.float32)
        total = total.astype(jnp.bfloat16)
        for block in range(GROUP):
            member, row = place_of(block)
            out_ref[member, row : row + PART, start : start + WIDE] = total[
                block * PART : (block + 1) * PART
            ]
    for block in range(GROUP):
        member, row = place_of(block)
        wide = x_ref[block].astype(jnp.float32)
        squares = jnp.sum(wide * wide, axis=1, keepdims=True)
        high = squares.astype(jnp.bfloat16).astype(jnp.float32)
        lane = lax.broadcasted_iota(jnp.int32, (PART, HD), 1)
        both = jnp.where(lane < HD // 2, high, squares - high)
        out_ref[member, row : row + PART, SQUARES:] = both.astype(jnp.bfloat16)


def project(x, *weights):
    return pl.pallas_call(
        project_kernel,
        out_shape=jax.ShapeDtypeStruct((4, TOK, SQUARES + HD), jnp.bfloat16),
        in_specs=in_vmem(5),
        out_specs=pl.BlockSpec(memory_space=pltpu.VMEM),
        compiler_params=pltpu.CompilerParams(vmem_limit_bytes=VMEM),
        cost_estimate=pl.CostEstimate(
            flops=3 * 2**30, bytes_accessed=9 * 2**20, transcendentals=0
        ),
    )(x, *weights)


def finish_kernel(core_ref, parts_ref, bias_ref, cos_ref, sin_ref, q_ref, kv_ref):
    core = core_ref[0]
    cosine = cos_ref[...]
    sine = sin_ref[...]

    def summed(start):
        total = parts_ref[0, :, start : start + HD].astype(jnp.float32)
        for part in range(1, 4):
            total = total + parts_ref[part, :, start : start + HD].astype(jnp.float32)
        return total

    squares = summed(SQUARES)
    ratio = lax.rsqrt((squares[:, :1] + squares[:, HD // 2 : HD // 2 + 1]) / D + EPSILON)
    for side in range(2):
        for column in range(5):
            start = side * WIDE + column * HD
            total = summed(start) * ratio + bias_ref[:, start : start + HD]
            turned = total * cosine + pltpu.roll(total, HD // 2, 1) * sine
            if column < 4:
                turned = (turned * QSCALE).astype(jnp.bfloat16)
                q_ref[0, side * 4 + column] = turned[:PART]
                q_ref[1, side * 4 + column] = turned[PART:]
            else:
                kind = core if side == 0 else 1 - core
                is_key = jnp.full(total.shape, kind, jnp.int32) == 0
                kv_ref[kind] = jnp.where(is_key, turned, total).astype(jnp.bfloat16)


def finish(core, parts, bias, cosine, sine):
    return pl.pallas_call(
        finish_kernel,
        out_shape=(
            jax.ShapeDtypeStruct((2, GROUP, PART, HD), jnp.bfloat16),
            jax.ShapeDtypeStruct((2, TOK, HD), jnp.bfloat16),
        ),
        in_specs=[pl.BlockSpec(memory_space=pltpu.SMEM)] + in_vmem(4),
        out_specs=tuple(in_vmem(2)),
        compiler_params=pltpu.CompilerParams(vmem_limit_bytes=VMEM),
    )(core, parts, bias, cosine, sine)


def with_ones(values):
    return jnp.concatenate([values, jnp.ones(values.shape, values.dtype)], axis=1)


def absorb(rows, query, keys, values, masks, peak_ref, acc_ref):
    scores = []
    for key, mask in zip(keys, masks, strict=True):
        score = lax.dot_general(
            query, key, (((1,), (1,)), ((), ())), preferred_element_type=jnp.float32
        )
        scores.append(score if mask is None else jnp.where(mask, score, LOWEST))
    old = peak_ref[rows, :]
    new = old
    for score in scores:
        new = jnp.maximum(new, jnp.max(score, axis=1, keepdims=True))
    fresh = None
    for score, value in zip(scores, values, strict=True):
        weights = jnp.exp2(score - new).astype(jnp.bfloat16)
        part = jnp.dot(weights, value, preferred_element_type=jnp.float32)
        fresh = part if fresh is None else fresh + part
    acc_ref[rows, :] = acc_ref[rows, :] * jnp.exp2(old - new) + fresh
    peak_ref[rows, :] = new


CHUNK = 256
ROWS = GROUP * TOK


def cache_kernel(distances, place_ref, q_ref, own_ref, peer_ref, acc_in, peak_in, acc_ref, peak_ref):
    offset = place_ref[0]
    core = place_ref[1]
    row = place_ref[2]
    if acc_in is None:
        acc_ref[...] = jnp.zeros_like(acc_ref)
        peak_ref[...] = jnp.full_like(peak_ref, LOWEST)
    else:
        acc_ref[...] = acc_in[...]
        peak_ref[...] = peak_in[...]

    def piece(index, carry):
        distance = distances[3]
        for at in range(3):
            distance = jnp.where(index == at, distances[at], distance)
        base = (row ^ distance) * SLOTS
        own_base = base + core * HALF
        peer_base = base + (1 - core) * HALF

        def step(masked):
            keys = [own_ref[index, 0], peer_ref[index, 0]]
            values = [with_ones(own_ref[index, 1]), with_ones(peer_ref[index, 1])]
            masks = [None, None]
            if masked:
                slot = lax.broadcasted_iota(jnp.int32, (CHUNK, HALF), 1)
                masks = [slot + own_base < offset, slot + peer_base < offset]
            for start in range(0, ROWS, CHUNK):
                rows = slice(start, start + CHUNK)
                absorb(rows, q_ref[rows, :], keys, values, masks, peak_ref, acc_ref)

        @pl.when(base + SLOTS <= offset)
        def _():
            step(False)

        @pl.when((base < offset) & (base + SLOTS > offset))
        def _():
            step(True)

        return carry

    lax.fori_loop(0, 4, piece, 0)


def first_cache_kernel(place_ref, q_ref, own_ref, peer_ref, acc_ref, peak_ref):
    cache_kernel(NEAR, place_ref, q_ref, own_ref, peer_ref, None, None, acc_ref, peak_ref)


def attend_cache(kernel, place, queries, own, peer, *state):
    return pl.pallas_call(
        kernel,
        out_shape=(
            jax.ShapeDtypeStruct((ROWS, 2 * HD), jnp.float32),
            jax.ShapeDtypeStruct((ROWS, 1), jnp.float32),
        ),
        in_specs=[pl.BlockSpec(memory_space=pltpu.SMEM)] + in_vmem(3 + len(state)),
        out_specs=tuple(in_vmem(2)),
        compiler_params=pltpu.CompilerParams(vmem_limit_bytes=VMEM),
        cost_estimate=pl.CostEstimate(
            flops=8 * 2**30, bytes_accessed=4 * 2**20, transcendentals=2**22
        ),
    )(place, queries, own, peer, *state)


def row_of(block, half):
    member, row = place_of(block)
    return MEMBERS[half][member], row


def span_kernel(
    place_ref, q_ref, own_ref, peer_ref, acc_in, peak_in, out_ref, acc_ref, peak_ref, k_ref, v_ref
):
    core = place_ref[1]
    half = place_ref[3]
    member = place_ref[4]
    acc_ref[...] = acc_in[...]
    peak_ref[...] = peak_in[...]
    v_ref[:, HD:] = jnp.ones((GROUP * 4 * PART, HD), jnp.bfloat16)
    for block in range(GROUP):
        for side, ref in enumerate((own_ref, peer_ref)):
            for part in range(2):
                device, row = row_of(block, part)
                start = block * 4 * PART + side * 2 * PART + part * PART
                k_ref[start : start + PART, :] = ref[device, 0, row : row + PART, :]
                v_ref[start : start + PART, :HD] = ref[device, 1, row : row + PART, :]
    width = GROUP * 2 * PART
    lane = lax.broadcasted_iota(jnp.int32, (CHUNK, width), 1)
    line = lax.broadcasted_iota(jnp.int32, (CHUNK, width), 0)
    within = lane % (2 * TOK)
    side_core = jnp.where(within < TOK, core, 1 - core)
    key_token = lane // (2 * TOK) * (2 * TOK) + side_core * TOK + within % TOK
    query_token = core * TOK + half * PART + line % PART
    for at in range(2):
        mine = member if at == 0 else 7 - member
        for begin in range(at * ROWS // 2, (at + 1) * ROWS // 2, CHUNK):
            rows = slice(begin, begin + CHUNK)
            keys, values, masks = [], [], []
            for first in range(0, (at + 1) * width, width):
                last = first == at * width
                keys.append(k_ref[first : first + width, :])
                values.append(v_ref[first : first + width, :])
                masks.append(
                    key_token + first <= query_token + mine * 2 * TOK if last else None
                )
            absorb(rows, q_ref[rows, :], keys, values, masks, peak_ref, acc_ref)
        for head in range(GROUP):
            first = at * ROWS // 2 + head * PART
            rows = slice(first, first + PART)
            out_ref[at * PART : (at + 1) * PART, head * HD : (head + 1) * HD] = (
                acc_ref[rows, :HD] / acc_ref[rows, HD:]
            ).astype(jnp.bfloat16)


def attend_span(place, queries, own, peer, acc, peak):
    return pl.pallas_call(
        span_kernel,
        out_shape=jax.ShapeDtypeStruct((TOK, GROUP * HD), jnp.bfloat16),
        in_specs=[pl.BlockSpec(memory_space=pltpu.SMEM)] + in_vmem(5),
        out_specs=pl.BlockSpec(memory_space=pltpu.VMEM),
        scratch_shapes=[
            pltpu.VMEM((ROWS, 2 * HD), jnp.float32),
            pltpu.VMEM((ROWS, 1), jnp.float32),
            pltpu.VMEM((GROUP * 4 * PART, HD), jnp.bfloat16),
            pltpu.VMEM((GROUP * 4 * PART, 2 * HD), jnp.bfloat16),
        ],
        compiler_params=pltpu.CompilerParams(vmem_limit_bytes=VMEM),
        cost_estimate=pl.CostEstimate(
            flops=3 * 2**30, bytes_accessed=4 * 2**20, transcendentals=2**21
        ),
    )(place, queries, own, peer, acc, peak)


def mix_kernel(a_ref, own_ref, peer_ref, own_x_ref, peer_x_ref, out_ref):
    a = a_ref[...].reshape(4 * TOK, GROUP * HD)
    width = 4 * HD
    for start, near, far in ((0, own_ref, peer_ref), (SLOTS, own_x_ref, peer_x_ref)):
        total = jnp.dot(a[:, :width], near[...], preferred_element_type=jnp.float32)
        total = total + jnp.dot(a[:, width:], far[...], preferred_element_type=jnp.float32)
        total = total.astype(jnp.bfloat16)
        for block in range(GROUP):
            member, row = place_of(block)
            row = row + member * TOK
            out_ref[block, :, start : start + SLOTS] = total[row : row + PART]


def mix(attended, *weights):
    return pl.pallas_call(
        mix_kernel,
        out_shape=jax.ShapeDtypeStruct((GROUP, PART, 2 * SLOTS), jnp.bfloat16),
        in_specs=in_vmem(5),
        out_specs=pl.BlockSpec(memory_space=pltpu.VMEM),
        compiler_params=pltpu.CompilerParams(vmem_limit_bytes=VMEM),
        cost_estimate=pl.CostEstimate(
            flops=2 * 2**30, bytes_accessed=7 * 2**20, transcendentals=0
        ),
    )(attended, *weights)


def body(
    hidden_in,
    norm_gain,
    w_query,
    scale_query,
    bias_query,
    w_keyval,
    scale_keyval,
    bias_keyval,
    w_out,
    scale_out,
    cache_keyval,
    span_offset,
):
    tie = lax.optimization_barrier
    row = lax.axis_index(ROW)
    x = lax.axis_index("x")
    head = lax.axis_index(COL)
    core = lax.axis_index("core")
    half = (x >> 1) ^ (x & 1)
    member = 2 * lax.axis_index("ylo") + (x >> 1)
    offset = span_offset[0]

    cached = lax.dynamic_slice(cache_keyval, (0, core * HALF, head * HD), (2, HALF, HD))
    cached_y = along(cached, "ylo", 2, 1)
    kept = lax.dynamic_slice_in_dim(hidden_in, half * PART, PART, 0)
    given = lax.dynamic_slice_in_dim(hidden_in, (1 - half) * PART, PART, 0)
    local = jnp.concatenate([kept, beside(given)], axis=1)
    local, cached_y = tie((local, cached_y))

    start = core * KVH + head
    weight = lax.dynamic_slice_in_dim(w_keyval, start * HD, HD, 1)
    scale = lax.dynamic_slice_in_dim(scale_keyval, start, 1, 1)
    weight = jnp.concatenate(
        [w_query.astype(jnp.float32) * expand(scale_query), weight.astype(jnp.float32) * expand(scale)],
        axis=1,
    )
    own = (weight * norm_gain[:, None]).astype(jnp.bfloat16)
    local, own = tie((local, own))
    gathered = exchange(copies(local, GROUP), COL)
    own_x = beside(own)
    peer = swap_cores(own)
    peer_x = swap_cores(own_x)

    bias = jnp.concatenate([bias_query, lax.dynamic_slice_in_dim(bias_keyval, start * HD, HD, 0)])
    bias = jnp.concatenate([bias, swap_cores(bias)])[None, :]

    pair = jnp.stack([cached, cached_y])
    near = jnp.concatenate([pair, along(pair, "x", 4, 3)], axis=0)
    near_peer = swap_cores(near)

    out_own = (w_out.astype(jnp.float32) * expand(scale_out)).astype(jnp.bfloat16)
    out_peer = swap_cores(out_own)

    index = jnp.arange(TOK, dtype=jnp.int32)
    block = jnp.where(index < PART, member, 7 - member)
    token = (2 * block + core) * TOK + half * PART + index % PART
    positions = (offset + token).astype(jnp.float32)
    inverse = ROPE_BASE ** (-(2.0 * jnp.arange(HD // 2, dtype=jnp.float32)) / HD)
    angles = positions[:, None] * inverse[None, :]
    cosine = jnp.cos(angles)
    sine = jnp.sin(angles)
    cosine = jnp.concatenate([cosine, cosine], axis=1)
    sine = jnp.concatenate([-sine, sine], axis=1)
    place = jnp.stack([offset, core, row, half, member]).astype(jnp.int32)

    near, own_x = tie((near, own_x))
    far = beside(near)
    gathered, bias, cosine, sine, place, out_own, out_peer, near_peer = tie(
        (gathered, bias, cosine, sine, place, out_own, out_peer, near_peer)
    )
    projected = project(gathered, own, own_x, peer, peer_x)
    parts = exchange(projected, ROW, MEMBERS)
    parts, out_own = tie((parts, out_own))
    out_own_x = beside(out_own)
    queries, own_kv = finish(place[1:2], parts, bias, cosine, sine)
    queries = queries.reshape(ROWS, HD)

    span_own = exchange(copies(own_kv, GROUP), ROW)
    state = attend_cache(first_cache_kernel, place, queries, near, near_peer)
    far_peer = swap_cores(far)
    span_own, state = tie((span_own, state))
    span_peer = swap_cores(span_own)
    state = attend_cache(
        functools.partial(cache_kernel, FAR), place, queries, far, far_peer, *state
    )
    attended = attend_span(place, queries, span_own, span_peer, *state)

    everyone = exchange(copies(attended, 4), ROW, MEMBERS)
    out_peer_x = swap_cores(out_own_x)
    mixed = mix(everyone, out_own, out_peer, out_own_x, out_peer_x)
    shares = exchange(mixed, COL)
    total = jnp.sum(shares.astype(jnp.float32), axis=0).astype(jnp.bfloat16)
    mine = total[:, :SLOTS]
    other = beside(total[:, SLOTS:])
    return jnp.where(
        half == 0, jnp.concatenate([mine, other]), jnp.concatenate([other, mine])
    )


def solution(mesh):
    fine = Mesh(mesh.devices.reshape(2, 4, 4, 2, 2), ("ylo", "x", "z", "yhi", "core"))
    row = ("ylo", "x")
    col = ("z", "yhi", "core")
    return jax.shard_map(
        body,
        mesh=fine,
        in_specs=(
            P(col, row),
            P(row),
            P(row, col),
            P(row, col),
            P(col),
            P(row, None),
            P(row, None),
            P(),
            P(col, row),
            P(col, row),
            P(None, row, None),
            P(),
        ),
        out_specs=P(col, row),
        check_vma=False,
    )
```

time: 240 us -> 190 us (0.79)
  waiting for transfers between devices: 94.1 us -> 57.8 us
  starting transfers between devices: 38.7 us -> 26 us
  Pallas kernels: 16 us -> 27 us
  matrix products: 9.47 us -> 0 us
  local copies, waits for them, and re-layouts: 19.7 us -> 15.7 us
  blocking collectives: 52.2 us -> 55.8 us
    all_to_all x4 -> x3, waiting for transfers between devices: 33.4 us -> 9.67 us  [exchange(): lax.all_to_all(array, axes, 0, 0, tiled=True, axis_index_groups=groups)]
    all_to_all x1 -> x2, blocking collectives: 33.2 us -> 55.8 us  [exchange(): lax.all_to_all(array, axes, 0, 0, tiled=True, axis_index_groups=groups)]
    psum x1 -> x0, blocking collectives: 19 us -> none  [body(): squares = lax.psum(jnp.sum(widened * widened, axis=1), ROW)]
    all_to_all x4 -> x3, starting transfers between devices: 28.6 us -> 15.9 us  [exchange(): lax.all_to_all(array, axes, 0, 0, tiled=True, axis_index_groups=groups)]
    ppermute x5 -> x7, waiting for transfers between devices: 58.1 us -> 47.3 us  [along(): return lax.ppermute(array, axis, [(i, i ^ distance) for i in range(size)])]
    dot_general x2 -> x0, matrix products: 9.47 us -> none  [the longest x1 5.92 us: body(): jnp.dot(gathered, weights, preferred_element_type=jnp.float32)]
    pallas_call x2 -> x5, Pallas kernels: 13.7 us -> 22.8 us  [the longest x2 8.89 us: attend_cache(): pl.pallas_call(kernel, out_shape=(jax.ShapeDtypeStruct((ROWS, 2 * HD), jn...]
    unnamed x26 -> x37, local copies, waits for them, and re-layouts: 9.13 us -> 6.36 us
  transfers between devices with their start and end apart: 15 -> 18, of which waited for: 6 -> 9; matrix products, arithmetic and copies ran while one was open for 10% -> 7% of each run, Pallas kernels for 6% -> 12%
where the time goes in v2:
time: 190 us; the launch traced here: 189 us
  waiting for transfers between devices  57.8 us (30%)
  blocking collectives  55.8 us (29%)
  Pallas kernels  27 us (14%)
  starting transfers between devices  26 us (14%)
  local copies, waits for them, and re-layouts  15.7 us (8%)
  other arithmetic  5.57 us (3%)
    all_to_all x2, blocking collectives, exchange(): lax.all_to_all(array, axes, 0, 0, tiled=True, axis_index_groups=groups)  55.8 us
    ppermute x7, waiting for transfers between devices, along(): return lax.ppermute(array, axis, [(i, i ^ distance) for i in range(size)])  47.3 us
    all_to_all x3, starting transfers between devices, exchange(): lax.all_to_all(array, axes, 0, 0, tiled=True, axis_index_groups=groups)  15.9 us
    all_to_all x3, waiting for transfers between devices, exchange(): lax.all_to_all(array, axes, 0, 0, tiled=True, axis_index_groups=groups)  9.67 us
    pallas_call x2, Pallas kernels, attend_cache(): pl.pallas_call(kernel, out_shape=(jax.ShapeDtypeStruct((ROWS, 2 * HD), jn...  8.89 us
    ppermute x7, starting transfers between devices, along(): return lax.ppermute(array, axis, [(i, i ^ distance) for i in range(size)])  8.89 us
    pallas_call x1, Pallas kernels, project(): pl.pallas_call(project_kernel, out_shape=jax.ShapeDtypeStruct((4, TOK, SQ...  7.55 us
    unnamed x37, local copies, waits for them, and re-layouts  6.36 us
  transfers between devices with their start and end apart: 18, of which 9 were waited for; matrix products, arithmetic and copies ran while one was open for 7% of the time, Pallas kernels for 12%

profile of v2, /device:TPU:0, one launch (start us, length us, event | category | flops | bytes accessed | tf_op | source)
XLA Modules:
  0.0 188.9 jit_solution(12973984191459046998)
XLA Ops:
  0.0 1.1 constant_dynamic-slice_fusion.2
  1.1 1.7 collective-permute-start
  2.7 1.0 constant_dynamic-slice_fusion
  3.7 1.7 collective-permute-start.1
  6.4 1.2 broadcast_in_dim.51
  8.1 1.2 convert_multiply_fusion
  9.5 2.0 %collective-permute-done.1 = bf16[2,512,128]{2,1,0:T(8,128)(2,1)S(1)} collective-permute-done((bf16[2,512,128]{2,1,0:T(8,128)(2,1)S(1)}, bf16[2,512,128]{2,1,0:T(8,128)(2,1)S(1)}, u32[]{:S(2)}, u32[]{:S(2)}) %collective-permute-start.1) | collective-permute-done | bytes 262176 | tf_op jit(solution)/shard_map/ppermute | solution.py:46
  11.9 1.0 fusion.9
  12.9 1.6 broadcast_in_dim.54
  14.5 8.2 %all-to-all-start = ((bf16[8,64,2048]{2,1,0:T(8,128)(2,1)}), bf16[8,64,2048]{2,1,0:T(8,128)(2,1)}, u32[]{:S(2)}, u32[]{:S(2)}) async-start(bf16[8,64,2048]{2,1,0:T(8,128)(2,1)} %broadcast_in_dim.54), calls=%async_computation | async-start | bytes 4194304 | tf_op jit(solution)/shard_map/all_to_all | solution.py:54
  22.9 2.8 %collective-permute-start.4 = (bf16[2,2,512,128]{3,2,1,0:T(8,128)(2,1)S(1)}, bf16[2,2,512,128]{3,2,1,0:T(8,128)(2,1)S(1)}, u32[]{:S(2)}, u32[]{:S(2)}) collective-permute-start(bf16[2,2,512,128]{3,2,1,0:T(8,128)(2,1)S(1)} %pad_maximum_fusion.1), channel_id=1, source_target_pairs={{0,48},{16,32},{32,16},{48,0},{1,49},{17,33},{33,17},{49,1},{2,50}... | collective-permute-start | bytes 1572872 | tf_op jit(solution)/shard_map/ppermute | solution.py:46
  25.7 15.3 %collective-permute-done.6.own_x_ref = bf16[1024,640]{1,0:T(8,128)(2,1)} collective-permute-done((bf16[1024,640]{1,0:T(8,128)(2,1)S(1)}, bf16[1024,640]{1,0:T(8,128)(2,1)}, u32[]{:S(2)}, u32[]{:S(2)}) %collective-permute-start.6) | collective-permute-done | bytes 1310752 | tf_op jit(solution)/shard_map/ppermute | solution.py:46
  48.2 1.6 all-to-all-done.x_ref
  49.9 7.5 %shard_map.118 = bf16[4,128,1408]{2,1,0:T(8,128)(2,1)} custom-call(bf16[8,64,2048]{2,1,0:T(8,128)(2,1)} %all-to-all-done.x_ref, bf16[1024,640]{1,0:T(8,128)(2,1)S(1)} %fusion.own_ref, bf16[1024,640]{1,0:T(8,128)(2,1)} %collective-permute-done.6.own_x_ref, bf16[1024,640]{1,0:T(8,128)(2,1)} %collective-permute-done.7.peer_ref, ...), custom_call_target="tpu_custom_call" | custom-call | flops 3221225472 | bytes 9437184 | tf_op jit(solution)/shard_map/pallas_call | solution.py:92
  57.4 4.1 %all-to-all-start.1 = ((bf16[4,128,1408]{2,1,0:T(8,128)(2,1)}), bf16[4,128,1408]{2,1,0:T(8,128)(2,1)S(1)}, u32[]{:S(2)}, u32[]{:S(2)}) async-start(bf16[4,128,1408]{2,1,0:T(8,128)(2,1)} %shard_map.118), calls=%async_computation.1 | async-start | bytes 2883584 | tf_op jit(solution)/shard_map/all_to_all | solution.py:54
  61.5 11.7 %collective-permute-done.10.own_ref = bf16[4,2,512,128]{3,2,1,0:T(8,128)(2,1)} collective-permute-done((bf16[4,2,512,128]{3,2,1,0:T(8,128)(2,1)S(1)}, bf16[4,2,512,128]{3,2,1,0:T(8,128)(2,1)}, u32[]{:S(2)}, u32[]{:S(2)}) %collective-permute-start.10) | collective-permute-done | bytes 1048608 | tf_op jit(solution)/shard_map/ppermute | solution.py:46
  73.9 6.3 %all-to-all-done.1.parts_ref = bf16[4,128,1408]{2,1,0:T(8,128)(2,1)S(1)} async-done(((bf16[4,128,1408]{2,1,0:T(8,128)(2,1)}), bf16[4,128,1408]{2,1,0:T(8,128)(2,1)S(1)}, u32[]{:S(2)}, u32[]{:S(2)}) %all-to-all-start.1) | async-done | bytes 1441824 | tf_op jit(solution)/shard_map/all_to_all | solution.py:54
  81.9 1.1 shard_map.119
  84.6 3.5 %all-to-all-start.2 = ((bf16[8,2,128,128]{3,2,1,0:T(8,128)(2,1)}), bf16[8,2,128,128]{3,2,1,0:T(8,128)(2,1)S(1)}, u32[]{:S(2)}, u32[]{:S(2)}) async-start(bf16[8,2,128,128]{3,2,1,0:T(8,128)(2,1)} %broadcast_in_dim.60), calls=%async_computation.2 | async-start | bytes 1048576 | tf_op jit(solution)/shard_map/all_to_all | solution.py:54
  88.1 1.9 %collective-permute-start.12 = (bf16[512,1024]{1,0:T(8,128)(2,1)S(1)}, bf16[512,1024]{1,0:T(8,128)(2,1)}, u32[]{:S(2)}, u32[]{:S(2)}) collective-permute-start(bf16[512,1024]{1,0:T(8,128)(2,1)S(1)} %fusion.1.own_ref), channel_id=1, source_target_pairs={{0,16},{16,0},{32,48},{48,32},{1,17},{17,1},{33,49},{49,33},{2,18}... | collective-permute-start | bytes 3145736 | tf_op jit(solution)/shard_map/ppermute | solution.py:46
  90.0 0.9 copy-done.4
  91.0 3.3 %shard_map.120 = (f32[1024,256]{1,0:T(8,128)S(1)}, f32[1024,1]{1,0:T(8,128)S(1)}) custom-call(s32[5]{0:T(128)S(1)} %stack.28.place_ref, bf16[1024,128]{1,0:T(8,128)(2,1)S(1)} %bitcast.22, bf16[4,2,512,128]{3,2,1,0:T(8,128)(2,1)S(1)} %pad_maximum_fusion.own_ref, bf16[4,2,512,128]{3,2,1,0:T(8,128)(2,1)} %collective-permute-done.5.peer_ref), custom_call_target="tpu_custom_call" | custom-call | flops 8589934592 | bytes 4194304 | tf_op jit(solution)/shard_map/pallas_call | solution.py:221
  94.3 1.0 copy-done.6
  95.3 1.8 all-to-all-done.2.own_ref
  97.1 1.3 copy-done.7
  98.4 5.5 %shard_map.121 = (f32[1024,256]{1,0:T(8,128)S(1)}, f32[1024,1]{1,0:T(8,128)S(1)}) custom-call(s32[5]{0:T(128)S(1)} %stack.28.place_ref, bf16[1024,128]{1,0:T(8,128)(2,1)S(1)} %bitcast.23, bf16[4,2,512,128]{3,2,1,0:T(8,128)(2,1)} %collective-permute-done.10.own_ref, bf16[4,2,512,128]{3,2,1,0:T(8,128)(2,1)} %collective-permute-done.11.peer_ref, ...), custom_call_target="tpu_custom_call" | custom-call | flops 8589934592 | bytes 4194304 | tf_op jit(solution)/shard_map/pallas_call | solution.py:221
  103.9 13.3 %collective-permute-done.12.own_x_ref = bf16[512,1024]{1,0:T(8,128)(2,1)} collective-permute-done((bf16[512,1024]{1,0:T(8,128)(2,1)S(1)}, bf16[512,1024]{1,0:T(8,128)(2,1)}, u32[]{:S(2)}, u32[]{:S(2)}) %collective-permute-start.12) | collective-permute-done | bytes 1048608 | tf_op jit(solution)/shard_map/ppermute | solution.py:46
  117.3 4.2 %shard_map.122 = bf16[128,1024]{1,0:T(8,128)(2,1)S(1)} custom-call(s32[5]{0:T(128)S(1)} %stack.28.place_ref, bf16[1024,128]{1,0:T(8,128)(2,1)S(1)} %bitcast.24, bf16[8,2,128,128]{3,2,1,0:T(8,128)(2,1)S(1)} %all-to-all-done.2.own_ref, bf16[8,2,128,128]{3,2,1,0:T(8,128)(2,1)S(1)} %collective-permute-done.9.peer_ref, f32[1024,256]{1,0:T(8,128)S(1)} %get-tuple-element.51.acc_in, ...), custom_call_target="tpu_custom_call" | custom-call | flops 3221225472 | bytes 4194304 | tf_op jit(solution)/shard_map/pallas_call | solution.py:286
  121.6 20.1 %all_to_all.25.a_ref = bf16[4,128,1024]{2,1,0:T(8,128)(2,1)S(1)} all-to-all(bf16[4,128,1024]{2,1,0:T(8,128)(2,1)S(1)} %broadcast_in_dim.61), channel_id=1, replica_groups={{0,48,64,112},{16,32,80,96},{1,49,65,113},{17,33,81,97},{2,50,66,114},{..., dimensions={0} | all-to-all | bytes 2097152 | tf_op jit(solution)/shard_map/all_to_all | solution.py:54
  141.7 5.2 %shard_map.123 = bf16[8,64,2048]{2,1,0:T(8,128)(2,1)} custom-call(bf16[4,128,1024]{2,1,0:T(8,128)(2,1)S(1)} %all_to_all.25.a_ref, bf16[512,1024]{1,0:T(8,128)(2,1)S(1)} %fusion.1.own_ref, bf16[512,1024]{1,0:T(8,128)(2,1)} %collective-permute-done.3.peer_ref, bf16[512,1024]{1,0:T(8,128)(2,1)} %collective-permute-done.12.own_x_ref, ...), custom_call_target="tpu_custom_call" | custom-call | flops 2147483648 | bytes 7340032 | tf_op jit(solution)/shard_map/pallas_call | solution.py:318
  147.0 35.7 %all_to_all.26 = bf16[8,64,2048]{2,1,0:T(8,128)(2,1)S(1)} all-to-all(bf16[8,64,2048]{2,1,0:T(8,128)(2,1)} %shard_map.123), channel_id=1, replica_groups=mesh['ylo'=2,'x'=4,'z'=4,'yhi'=2,'core'=2] {'z','yhi'}, dimensions={0} | all-to-all | bytes 4194304 | tf_op jit(solution)/shard_map/all_to_all | solution.py:54
  183.2 4.9 %collective-permute-done.14 = bf16[64,1024]{1,0:T(8,128)(2,1)S(1)} collective-permute-done((bf16[64,1024]{1,0:T(8,128)(2,1)S(1)}, bf16[64,1024]{1,0:T(8,128)(2,1)S(1)}, u32[]{:S(2)}, u32[]{:S(2)}) %collective-permute-start.14) | collective-permute-done | bytes 131104 | tf_op jit(solution)/shard_map/ppermute | solution.py:46
  (81 shorter events, 13.9 us)
Async XLA Ops:
  0.0 5.4 %copy-start = (f32[8,16]{1,0:T(8,128)S(1)}, f32[8,16]{1,0:T(8,128)}, u32[]{:S(2)}) copy-start(f32[8,16]{1,0:T(8,128)} %param.18) | copy-start | bytes 1540
  0.0 7.7 %copy-start.10 = (bf16[1024,512]{1,0:T(8,128)(2,1)S(1)}, bf16[1024,512]{1,0:T(8,128)(2,1)}, u32[]{:S(2)}) copy-start(bf16[1024,512]{1,0:T(8,128)(2,1)} %param.14) | copy-start | bytes 3145732
  1.1 8.4 %collective-permute-start = (bf16[64,1024]{1,0:T(8,128)(2,1)S(1)}, bf16[64,1024]{1,0:T(8,128)(2,1)S(1)}, u32[]{:S(2)}, u32[]{:S(2)}) collective-permute-start(bf16[64,1024]{1,0:T(8,128)(2,1)S(1)} %get-tuple-element.58), channel_id=1, source_target_pairs={{0,16},{16,0},{32,48},{48,32},{1,17},{17,1},{33,49},{49,33},{2,18}... | collective-permute-start | bytes 393224 | tf_op jit(solution)/shard_map/ppermute | solution.py:46
  3.7 7.8 %collective-permute-start.1 = (bf16[2,512,128]{2,1,0:T(8,128)(2,1)S(1)}, bf16[2,512,128]{2,1,0:T(8,128)(2,1)S(1)}, u32[]{:S(2)}, u32[]{:S(2)}) collective-permute-start(bf16[2,512,128]{2,1,0:T(8,128)(2,1)S(1)} %constant_dynamic-slice_fusion), channel_id=1, source_target_pairs={{0,64},{64,0},{1,65},{65,1},{2,66},{66,2},{3,67},{67,3},{4,68},{68... | collective-permute-start | bytes 786440 | tf_op jit(solution)/shard_map/ppermute | solution.py:46
  7.7 1.6 copy-start.15
  11.6 11.2 %copy-start.12 = (bf16[2,512,128]{2,1,0:T(8,128)(2,1)}, bf16[2,512,128]{2,1,0:T(8,128)(2,1)S(1)}, u32[]{:S(2)}) copy-start(bf16[2,512,128]{2,1,0:T(8,128)(2,1)S(1)} %collective-permute-done.1) | copy-start | bytes 786436
  11.6 29.4 %collective-permute-start.6 = (bf16[1024,640]{1,0:T(8,128)(2,1)S(1)}, bf16[1024,640]{1,0:T(8,128)(2,1)}, u32[]{:S(2)}, u32[]{:S(2)}) collective-permute-start(bf16[1024,640]{1,0:T(8,128)(2,1)S(1)} %fusion.own_ref), channel_id=1, source_target_pairs={{0,16},{16,0},{32,48},{48,32},{1,17},{17,1},{33,49},{49,33},{2,18}... | collective-permute-start | bytes 3932168 | tf_op jit(solution)/shard_map/ppermute | solution.py:46
  12.9 9.9 %copy-start.8 = (bf16[1,2,512,128]{3,2,1,0:T(8,128)(2,1)}, bf16[1,2,512,128]{3,2,1,0:T(8,128)(2,1)S(1)}, u32[]{:S(2)}) copy-start(bf16[1,2,512,128]{3,2,1,0:T(8,128)(2,1)S(1)} %fusion.9) | copy-start | bytes 786436
  14.5 26.5 %copy-start.16 = (f32[4,8]{1,0:T(4,128)S(1)}, f32[4,8]{1,0:T(4,128)}, u32[]{:S(2)}) copy-start(f32[4,8]{1,0:T(4,128)} %param.21) | copy-start | bytes 388
  14.5 35.3 %all-to-all-start = ((bf16[8,64,2048]{2,1,0:T(8,128)(2,1)}), bf16[8,64,2048]{2,1,0:T(8,128)(2,1)}, u32[]{:S(2)}, u32[]{:S(2)}) async-start(bf16[8,64,2048]{2,1,0:T(8,128)(2,1)} %broadcast_in_dim.54), calls=%async_computation | async-start | bytes 4194304 | tf_op jit(solution)/shard_map/all_to_all | solution.py:54
  22.8 18.9 %copy-start.11 = (bf16[512,1024]{1,0:T(8,128)(2,1)S(1)}, bf16[512,1024]{1,0:T(8,128)(2,1)}, u32[]{:S(2)}) copy-start(bf16[512,1024]{1,0:T(8,128)(2,1)} %param.20) | copy-start | bytes 3145732
  22.9 20.1 %collective-permute-start.4 = (bf16[2,2,512,128]{3,2,1,0:T(8,128)(2,1)S(1)}, bf16[2,2,512,128]{3,2,1,0:T(8,128)(2,1)S(1)}, u32[]{:S(2)}, u32[]{:S(2)}) collective-permute-start(bf16[2,2,512,128]{3,2,1,0:T(8,128)(2,1)S(1)} %pad_maximum_fusion.1), channel_id=1, source_target_pairs={{0,48},{16,32},{32,16},{48,0},{1,49},{17,33},{33,17},{49,1},{2,50}... | collective-permute-start | bytes 1572872 | tf_op jit(solution)/shard_map/ppermute | solution.py:46
  25.7 24.2 %collective-permute-start.7 = (bf16[1024,640]{1,0:T(8,128)(2,1)S(1)}, bf16[1024,640]{1,0:T(8,128)(2,1)}, u32[]{:S(2)}, u32[]{:S(2)}) collective-permute-start(bf16[1024,640]{1,0:T(8,128)(2,1)S(1)} %fusion.own_ref), channel_id=1, source_target_pairs={{0,1},{1,0},{2,3},{3,2},{4,5},{5,4},{6,7},{7,6},{8,9},{9,8},{10,11... | collective-permute-start | bytes 3932168 | tf_op jit(solution)/shard_map/ppermute | solution.py:42
  41.0 8.9 %collective-permute-start.8 = (bf16[1024,640]{1,0:T(8,128)(2,1)}, bf16[1024,640]{1,0:T(8,128)(2,1)}, u32[]{:S(2)}, u32[]{:S(2)}) collective-permute-start(bf16[1024,640]{1,0:T(8,128)(2,1)} %collective-permute-done.6.own_x_ref), channel_id=1, source_target_pairs={{0,1},{1,0},{2,3},{3,2},{4,5},{5,4},{6,7},{7,6},{8,9},{9,8},{10,11... | collective-permute-start | bytes 3932168 | tf_op jit(solution)/shard_map/ppermute | solution.py:42
  41.6 1.4 copy-start.9
  41.7 1.4 copy-start.13
  42.4 1.7 copy-start.14
  42.4 5.8 %collective-permute-start.3 = (bf16[512,1024]{1,0:T(8,128)(2,1)S(1)}, bf16[512,1024]{1,0:T(8,128)(2,1)}, u32[]{:S(2)}, u32[]{:S(2)}) collective-permute-start(bf16[512,1024]{1,0:T(8,128)(2,1)S(1)} %fusion.1.own_ref), channel_id=1, source_target_pairs={{0,1},{1,0},{2,3},{3,2},{4,5},{5,4},{6,7},{7,6},{8,9},{9,8},{10,11... | collective-permute-start | bytes 3145736 | tf_op jit(solution)/shard_map/ppermute | solution.py:42
  43.1 5.1 %collective-permute-start.5 = (bf16[4,2,512,128]{3,2,1,0:T(8,128)(2,1)S(1)}, bf16[4,2,512,128]{3,2,1,0:T(8,128)(2,1)}, u32[]{:S(2)}, u32[]{:S(2)}) collective-permute-start(bf16[4,2,512,128]{3,2,1,0:T(8,128)(2,1)S(1)} %pad_maximum_fusion.own_ref), channel_id=1, source_target_pairs={{0,1},{1,0},{2,3},{3,2},{4,5},{5,4},{6,7},{7,6},{8,9},{9,8},{10,11... | collective-permute-start | bytes 3145736 | tf_op jit(solution)/shard_map/ppermute | solution.py:42
  44.1 1.1 copy-start.17
  44.1 3.0 %collective-permute-start.2 = (f32[640]{0:T(1024)S(1)}, f32[640]{0:T(1024)}, u32[]{:S(2)}, u32[]{:S(2)}) collective-permute-start(f32[640]{0:T(1024)S(1)} %pad_maximum_fusion.6), channel_id=1, source_target_pairs={{0,1},{1,0},{2,3},{3,2},{4,5},{5,4},{6,7},{7,6},{8,9},{9,8},{10,11... | collective-permute-start | bytes 7688 | tf_op jit(solution)/shard_map/ppermute | solution.py:42
  47.9 25.4 %collective-permute-start.10 = (bf16[4,2,512,128]{3,2,1,0:T(8,128)(2,1)S(1)}, bf16[4,2,512,128]{3,2,1,0:T(8,128)(2,1)}, u32[]{:S(2)}, u32[]{:S(2)}) collective-permute-start(bf16[4,2,512,128]{3,2,1,0:T(8,128)(2,1)S(1)} %pad_maximum_fusion.own_ref), channel_id=1, source_target_pairs={{0,16},{16,0},{32,48},{48,32},{1,17},{17,1},{33,49},{49,33},{2,18}... | collective-permute-start | bytes 3145736 | tf_op jit(solution)/shard_map/ppermute | solution.py:46
  57.4 22.8 %all-to-all-start.1 = ((bf16[4,128,1408]{2,1,0:T(8,128)(2,1)}), bf16[4,128,1408]{2,1,0:T(8,128)(2,1)S(1)}, u32[]{:S(2)}, u32[]{:S(2)}) async-start(bf16[4,128,1408]{2,1,0:T(8,128)(2,1)} %shard_map.118), calls=%async_computation.1 | async-start | bytes 2883584 | tf_op jit(solution)/shard_map/all_to_all | solution.py:54
  73.3 23.8 %collective-permute-start.11 = (bf16[4,2,512,128]{3,2,1,0:T(8,128)(2,1)}, bf16[4,2,512,128]{3,2,1,0:T(8,128)(2,1)}, u32[]{:S(2)}, u32[]{:S(2)}) collective-permute-start(bf16[4,2,512,128]{3,2,1,0:T(8,128)(2,1)} %collective-permute-done.10.own_ref), channel_id=1, source_target_pairs={{0,1},{1,0},{2,3},{3,2},{4,5},{5,4},{6,7},{7,6},{8,9},{9,8},{10,11... | collective-permute-start | bytes 3145736 | tf_op jit(solution)/shard_map/ppermute | solution.py:42
  84.6 12.5 %all-to-all-start.2 = ((bf16[8,2,128,128]{3,2,1,0:T(8,128)(2,1)}), bf16[8,2,128,128]{3,2,1,0:T(8,128)(2,1)S(1)}, u32[]{:S(2)}, u32[]{:S(2)}) async-start(bf16[8,2,128,128]{3,2,1,0:T(8,128)(2,1)} %broadcast_in_dim.60), calls=%async_computation.2 | async-start | bytes 1048576 | tf_op jit(solution)/shard_map/all_to_all | solution.py:54
  88.1 29.1 %collective-permute-start.12 = (bf16[512,1024]{1,0:T(8,128)(2,1)S(1)}, bf16[512,1024]{1,0:T(8,128)(2,1)}, u32[]{:S(2)}, u32[]{:S(2)}) collective-permute-start(bf16[512,1024]{1,0:T(8,128)(2,1)S(1)} %fusion.1.own_ref), channel_id=1, source_target_pairs={{0,16},{16,0},{32,48},{48,32},{1,17},{17,1},{33,49},{49,33},{2,18}... | collective-permute-start | bytes 3145736 | tf_op jit(solution)/shard_map/ppermute | solution.py:46
  94.3 1.0 copy-start.6
  97.1 20.2 %copy-start.5 = (bf16[2,8,64,128]{3,2,1,0:T(8,128)(2,1)S(1)}, bf16[2,8,64,128]{3,2,1,0:T(8,128)(2,1)}, u32[]{:S(2)}) copy-start(bf16[2,8,64,128]{3,2,1,0:T(8,128)(2,1)} %copy-done.3) | copy-start | bytes 786436
  97.1 20.2 %collective-permute-start.9 = (bf16[8,2,128,128]{3,2,1,0:T(8,128)(2,1)S(1)}, bf16[8,2,128,128]{3,2,1,0:T(8,128)(2,1)S(1)}, u32[]{:S(2)}, u32[]{:S(2)}) collective-permute-start(bf16[8,2,128,128]{3,2,1,0:T(8,128)(2,1)S(1)} %all-to-all-done.2.own_ref), channel_id=1, source_target_pairs={{0,1},{1,0},{2,3},{3,2},{4,5},{5,4},{6,7},{7,6},{8,9},{9,8},{10,11... | collective-permute-start | bytes 1572872 | tf_op jit(solution)/shard_map/ppermute | solution.py:42
  97.1 1.3 copy-start.7
  117.3 24.5 %collective-permute-start.13 = (bf16[512,1024]{1,0:T(8,128)(2,1)}, bf16[512,1024]{1,0:T(8,128)(2,1)S(1)}, u32[]{:S(2)}, u32[]{:S(2)}) collective-permute-start(bf16[512,1024]{1,0:T(8,128)(2,1)} %collective-permute-done.12.own_x_ref), channel_id=1, source_target_pairs={{0,1},{1,0},{2,3},{3,2},{4,5},{5,4},{6,7},{7,6},{8,9},{9,8},{10,11... | collective-permute-start | bytes 3145736 | tf_op jit(solution)/shard_map/ppermute | solution.py:42
  183.1 5.0 %collective-permute-start.14 = (bf16[64,1024]{1,0:T(8,128)(2,1)S(1)}, bf16[64,1024]{1,0:T(8,128)(2,1)S(1)}, u32[]{:S(2)}, u32[]{:S(2)}) collective-permute-start(bf16[64,1024]{1,0:T(8,128)(2,1)S(1)} %get-tuple-element.56), channel_id=1, source_target_pairs={{0,16},{16,0},{32,48},{48,32},{1,17},{17,1},{33,49},{49,33},{2,18}... | collective-permute-start | bytes 393224 | tf_op jit(solution)/shard_map/ppermute | solution.py:46
  (4 other events, 3.3 us)

commit v3 on v2

--- a/solution.py
+++ b/solution.py
@@ -1,4 +1,3 @@
-import functools
 import math
 
 import jax
@@ -31,7 +30,7 @@
 NEAR = (0, 4, 3, 7)
 FAR = (1, 5, 2, 6)
 MEMBERS = ((0, 3, 4, 7), (1, 2, 5, 6))
-VMEM = 48 * 2**20
+VMEM = 26 * 2**20
 
 
 def expand(block_scale):
@@ -101,10 +100,13 @@
     )(x, *weights)
 
 
-def finish_kernel(core_ref, parts_ref, bias_ref, cos_ref, sin_ref, q_ref, kv_ref):
+def finish_kernel(core_ref, parts_ref, bias_ref, turns_ref, q_ref, kv_ref):
     core = core_ref[0]
-    cosine = cos_ref[...]
-    sine = sin_ref[...]
+    turns = turns_ref[...]
+    turned_turns = pltpu.roll(turns, HD // 2, 1)
+    low = lax.broadcasted_iota(jnp.int32, turns.shape, 1) < HD // 2
+    cosine = jnp.where(low, turns, turned_turns)
+    sine = jnp.where(low, -turned_turns, turns)
 
     def summed(start):
         total = parts_ref[0, :, start : start + HD].astype(jnp.float32)
@@ -129,17 +131,17 @@
                 kv_ref[kind] = jnp.where(is_key, turned, total).astype(jnp.bfloat16)
 
 
-def finish(core, parts, bias, cosine, sine):
+def finish(core, parts, bias, turns):
     return pl.pallas_call(
         finish_kernel,
         out_shape=(
             jax.ShapeDtypeStruct((2, GROUP, PART, HD), jnp.bfloat16),
             jax.ShapeDtypeStruct((2, TOK, HD), jnp.bfloat16),
         ),
-        in_specs=[pl.BlockSpec(memory_space=pltpu.SMEM)] + in_vmem(4),
+        in_specs=[pl.BlockSpec(memory_space=pltpu.SMEM)] + in_vmem(3),
         out_specs=tuple(in_vmem(2)),
         compiler_params=pltpu.CompilerParams(vmem_limit_bytes=VMEM),
-    )(core, parts, bias, cosine, sine)
+    )(core, parts, bias, turns)
 
 
 def with_ones(values):
@@ -166,32 +168,58 @@
     peak_ref[rows, :] = new
 
 
-CHUNK = 256
+CHUNK = 128
 ROWS = GROUP * TOK
 
 
-def cache_kernel(distances, place_ref, q_ref, own_ref, peer_ref, acc_in, peak_in, acc_ref, peak_ref):
+def cache_kernel(
+    place_ref,
+    q_ref,
+    near_own,
+    near_peer,
+    far_own,
+    far_peer,
+    acc_ref,
+    peak_ref,
+    own_ref,
+    peer_ref,
+    sems,
+):
     offset = place_ref[0]
     core = place_ref[1]
     row = place_ref[2]
-    if acc_in is None:
-        acc_ref[...] = jnp.zeros_like(acc_ref)
-        peak_ref[...] = jnp.full_like(peak_ref, LOWEST)
-    else:
-        acc_ref[...] = acc_in[...]
-        peak_ref[...] = peak_in[...]
-
-    def piece(index, carry):
+    groups = ((NEAR, near_own, near_peer), (FAR, far_own, far_peer))
+
+    def fetch(group, index):
+        own_hbm, peer_hbm = groups[group][1:]
+        at = group * 4 + index
+        return (
+            pltpu.make_async_copy(own_hbm.at[index], own_ref.at[at], sems.at[0, at]),
+            pltpu.make_async_copy(peer_hbm.at[index], peer_ref.at[at], sems.at[1, at]),
+        )
+
+    for group in range(2):
+        for index in range(4):
+            for copy in fetch(group, index):
+                copy.start()
+    acc_ref[...] = jnp.zeros_like(acc_ref)
+    peak_ref[...] = jnp.full_like(peak_ref, LOWEST)
+
+    def piece(group, index):
+        distances = groups[group][0]
         distance = distances[3]
         for at in range(3):
             distance = jnp.where(index == at, distances[at], distance)
+        for copy in fetch(group, index):
+            copy.wait()
+        held = group * 4 + index
         base = (row ^ distance) * SLOTS
         own_base = base + core * HALF
         peer_base = base + (1 - core) * HALF
 
         def step(masked):
-            keys = [own_ref[index, 0], peer_ref[index, 0]]
-            values = [with_ones(own_ref[index, 1]), with_ones(peer_ref[index, 1])]
+            keys = [own_ref[held, 0], peer_ref[held, 0]]
+            values = [with_ones(own_ref[held, 1]), with_ones(peer_ref[held, 1])]
             masks = [None, None]
             if masked:
                 slot = lax.broadcasted_iota(jnp.int32, (CHUNK, HALF), 1)
@@ -208,29 +236,36 @@
         def _():
             step(True)
 
-        return carry
-
-    lax.fori_loop(0, 4, piece, 0)
-
-
-def first_cache_kernel(place_ref, q_ref, own_ref, peer_ref, acc_ref, peak_ref):
-    cache_kernel(NEAR, place_ref, q_ref, own_ref, peer_ref, None, None, acc_ref, peak_ref)
-
-
-def attend_cache(kernel, place, queries, own, peer, *state):
+    for group in range(2):
+
+        def one(index, carry, group=group):
+            piece(group, index)
+            return carry
+
+        lax.fori_loop(0, 4, one, 0)
+
+
+def attend_cache(place, queries, *pieces):
     return pl.pallas_call(
-        kernel,
+        cache_kernel,
         out_shape=(
             jax.ShapeDtypeStruct((ROWS, 2 * HD), jnp.float32),
             jax.ShapeDtypeStruct((ROWS, 1), jnp.float32),
         ),
-        in_specs=[pl.BlockSpec(memory_space=pltpu.SMEM)] + in_vmem(3 + len(state)),
+        in_specs=[pl.BlockSpec(memory_space=pltpu.SMEM)]
+        + in_vmem(1)
+        + [pl.BlockSpec(memory_space=pl.ANY)] * 4,
         out_specs=tuple(in_vmem(2)),
+        scratch_shapes=[
+            pltpu.VMEM((8, 2, HALF, HD), jnp.bfloat16),
+            pltpu.VMEM((8, 2, HALF, HD), jnp.bfloat16),
+            pltpu.SemaphoreType.DMA((2, 8)),
+        ],
         compiler_params=pltpu.CompilerParams(vmem_limit_bytes=VMEM),
         cost_estimate=pl.CostEstimate(
-            flops=8 * 2**30, bytes_accessed=4 * 2**20, transcendentals=2**22
-        ),
-    )(place, queries, own, peer, *state)
+            flops=16 * 2**30, bytes_accessed=8 * 2**20, transcendentals=2**23
+        ),
+    )(place, queries, *pieces)
 
 
 def row_of(block, half):
@@ -239,7 +274,7 @@
 
 
 def span_kernel(
-    place_ref, q_ref, own_ref, peer_ref, acc_in, peak_in, out_ref, acc_ref, peak_ref, k_ref, v_ref
+    place_ref, q_ref, span_ref, acc_in, peak_in, out_ref, acc_ref, peak_ref, k_ref, v_ref
 ):
     core = place_ref[1]
     half = place_ref[3]
@@ -248,12 +283,12 @@
     peak_ref[...] = peak_in[...]
     v_ref[:, HD:] = jnp.ones((GROUP * 4 * PART, HD), jnp.bfloat16)
     for block in range(GROUP):
-        for side, ref in enumerate((own_ref, peer_ref)):
+        for side in range(2):
             for part in range(2):
                 device, row = row_of(block, part)
                 start = block * 4 * PART + side * 2 * PART + part * PART
-                k_ref[start : start + PART, :] = ref[device, 0, row : row + PART, :]
-                v_ref[start : start + PART, :HD] = ref[device, 1, row : row + PART, :]
+                k_ref[start : start + PART, :] = span_ref[device, side, 0, row : row + PART, :]
+                v_ref[start : start + PART, :HD] = span_ref[device, side, 1, row : row + PART, :]
     width = GROUP * 2 * PART
     lane = lax.broadcasted_iota(jnp.int32, (CHUNK, width), 1)
     line = lax.broadcasted_iota(jnp.int32, (CHUNK, width), 0)
@@ -282,11 +317,11 @@
             ).astype(jnp.bfloat16)
 
 
-def attend_span(place, queries, own, peer, acc, peak):
+def attend_span(place, queries, span, acc, peak):
     return pl.pallas_call(
         span_kernel,
         out_shape=jax.ShapeDtypeStruct((TOK, GROUP * HD), jnp.bfloat16),
-        in_specs=[pl.BlockSpec(memory_space=pltpu.SMEM)] + in_vmem(5),
+        in_specs=[pl.BlockSpec(memory_space=pltpu.SMEM)] + in_vmem(4),
         out_specs=pl.BlockSpec(memory_space=pltpu.VMEM),
         scratch_shapes=[
             pltpu.VMEM((ROWS, 2 * HD), jnp.float32),
@@ -298,7 +333,7 @@
         cost_estimate=pl.CostEstimate(
             flops=3 * 2**30, bytes_accessed=4 * 2**20, transcendentals=2**21
         ),
-    )(place, queries, own, peer, acc, peak)
+    )(place, queries, span, acc, peak)
 
 
 def mix_kernel(a_ref, own_ref, peer_ref, own_x_ref, peer_x_ref, out_ref):
@@ -356,6 +391,7 @@
     given = lax.dynamic_slice_in_dim(hidden_in, (1 - half) * PART, PART, 0)
     local = jnp.concatenate([kept, beside(given)], axis=1)
     local, cached_y = tie((local, cached_y))
+    gathered = exchange(copies(local, GROUP), COL)
 
     start = core * KVH + head
     weight = lax.dynamic_slice_in_dim(w_keyval, start * HD, HD, 1)
@@ -366,7 +402,6 @@
     )
     own = (weight * norm_gain[:, None]).astype(jnp.bfloat16)
     local, own = tie((local, own))
-    gathered = exchange(copies(local, GROUP), COL)
     own_x = beside(own)
     peer = swap_cores(own)
     peer_x = swap_cores(own_x)
@@ -387,35 +422,29 @@
     positions = (offset + token).astype(jnp.float32)
     inverse = ROPE_BASE ** (-(2.0 * jnp.arange(HD // 2, dtype=jnp.float32)) / HD)
     angles = positions[:, None] * inverse[None, :]
-    cosine = jnp.cos(angles)
-    sine = jnp.sin(angles)
-    cosine = jnp.concatenate([cosine, cosine], axis=1)
-    sine = jnp.concatenate([-sine, sine], axis=1)
+    turns = jnp.concatenate([jnp.cos(angles), jnp.sin(angles)], axis=1)
     place = jnp.stack([offset, core, row, half, member]).astype(jnp.int32)
 
     near, own_x = tie((near, own_x))
     far = beside(near)
-    gathered, bias, cosine, sine, place, out_own, out_peer, near_peer = tie(
-        (gathered, bias, cosine, sine, place, out_own, out_peer, near_peer)
+    gathered, bias, turns, place, out_own, out_peer, near_peer = tie(
+        (gathered, bias, turns, place, out_own, out_peer, near_peer)
     )
     projected = project(gathered, own, own_x, peer, peer_x)
     parts = exchange(projected, ROW, MEMBERS)
-    parts, out_own = tie((parts, out_own))
+    queries, own_kv = finish(place[1:2], parts, bias, turns)
+    queries = queries.reshape(ROWS, HD)
+
+    pair_kv = jnp.stack([own_kv, swap_cores(own_kv)])
+    queries, pair_kv = tie((queries, copies(pair_kv, GROUP)))
+    span = exchange(pair_kv, ROW)
+    state = attend_cache(place, queries, near, near_peer, far, swap_cores(far))
+    state, span, out_own = tie((state, span, out_own))
     out_own_x = beside(out_own)
-    queries, own_kv = finish(place[1:2], parts, bias, cosine, sine)
-    queries = queries.reshape(ROWS, HD)
-
-    span_own = exchange(copies(own_kv, GROUP), ROW)
-    state = attend_cache(first_cache_kernel, place, queries, near, near_peer)
-    far_peer = swap_cores(far)
-    span_own, state = tie((span_own, state))
-    span_peer = swap_cores(span_own)
-    state = attend_cache(
-        functools.partial(cache_kernel, FAR), place, queries, far, far_peer, *state
-    )
-    attended = attend_span(place, queries, span_own, span_peer, *state)
+    attended = attend_span(place, queries, span, *state)
 
     everyone = exchange(copies(attended, 4), ROW, MEMBERS)
+    everyone, out_own_x = tie((everyone, out_own_x))
     out_peer_x = swap_cores(out_own_x)
     mixed = mix(everyone, out_own, out_peer, out_own_x, out_peer_x)
     shares = exchange(mixed, COL)

time: 190 us -> 178 us (0.937)
  waiting for transfers between devices: 57.8 us -> 50 us
  local copies, waits for them, and re-layouts: 15.7 us -> 13.3 us
  blocking collectives: 55.8 us -> 53.5 us
    ppermute x7, waiting for transfers between devices: 47.3 us -> 33.4 us  [along(): return lax.ppermute(array, axis, [(i, i ^ distance) for i in range(size)])]
    ppermute x8, waiting for transfers between devices: 0.77 us -> 4.46 us  [swap_cores(): return lax.ppermute(array, 'core', [(0, 1), (1, 0)])]
    unnamed x37 -> x23, local copies, waits for them, and re-layouts: 6.36 us -> 2.98 us
    all_to_all x3, waiting for transfers between devices: 9.67 us -> 12.1 us  [exchange(): lax.all_to_all(array, axes, 0, 0, tiled=True, axis_index_groups=groups)]
    all_to_all x2, blocking collectives: 55.8 us -> 53.5 us  [exchange(): lax.all_to_all(array, axes, 0, 0, tiled=True, axis_index_groups=groups)]
    pallas_call x2 -> x1, Pallas kernels: 8.89 us -> 11 us  [attend_cache(): pl.pallas_call(cache_kernel, out_shape=(jax.ShapeDtypeStruct((ROWS, 2 * H...]
  transfers between devices with their start and end apart: 18 -> 18, of which waited for: 9 -> 11; matrix products, arithmetic and copies ran while one was open for 7% -> 9% of each run, Pallas kernels for 12% -> 13%
where the time goes in v3:
time: 178 us; the launch traced here: 177 us
  blocking collectives  53.5 us (30%)
  waiting for transfers between devices  50 us (28%)
  Pallas kernels  26.9 us (15%)
  starting transfers between devices  25.5 us (14%)
  local copies, waits for them, and re-layouts  13.3 us (7%)
  other arithmetic  7.26 us (4%)
    all_to_all x2, blocking collectives, exchange(): lax.all_to_all(array, axes, 0, 0, tiled=True, axis_index_groups=groups)  53.5 us
    ppermute x7, waiting for transfers between devices, along(): return lax.ppermute(array, axis, [(i, i ^ distance) for i in range(size)])  33.4 us
    all_to_all x3, starting transfers between devices, exchange(): lax.all_to_all(array, axes, 0, 0, tiled=True, axis_index_groups=groups)  16.1 us
    all_to_all x3, waiting for transfers between devices, exchange(): lax.all_to_all(array, axes, 0, 0, tiled=True, axis_index_groups=groups)  12.1 us
    pallas_call x1, Pallas kernels, attend_cache(): pl.pallas_call(cache_kernel, out_shape=(jax.ShapeDtypeStruct((ROWS, 2 * H...  11 us
    ppermute x7, starting transfers between devices, along(): return lax.ppermute(array, axis, [(i, i ^ distance) for i in range(size)])  8.16 us
    pallas_call x1, Pallas kernels, project(): pl.pallas_call(project_kernel, out_shape=jax.ShapeDtypeStruct((4, TOK, SQ...  6.94 us
    ppermute x8, waiting for transfers between devices, swap_cores(): return lax.ppermute(array, 'core', [(0, 1), (1, 0)])  4.46 us
  transfers between devices with their start and end apart: 18, of which 11 were waited for; matrix products, arithmetic and copies ran while one was open for 9% of the time, Pallas kernels for 13%

profile of v3, /device:TPU:0, one launch (start us, length us, event | category | flops | bytes accessed | tf_op | source)
XLA Modules:
  0.0 177.4 jit_solution(1326599599353199166)
XLA Ops:
  1.1 1.7 collective-permute-start
  3.7 1.7 collective-permute-start.1
  6.4 1.2 broadcast_in_dim.57
  8.1 1.2 convert_multiply_fusion
  9.5 2.0 %collective-permute-done.1 = bf16[2,512,128]{2,1,0:T(8,128)(2,1)S(1)} collective-permute-done((bf16[2,512,128]{2,1,0:T(8,128)(2,1)S(1)}, bf16[2,512,128]{2,1,0:T(8,128)(2,1)S(1)}, u32[]{:S(2)}, u32[]{:S(2)}) %collective-permute-start.1) | collective-permute-done | bytes 262176 | tf_op jit(solution)/shard_map/ppermute | solution.py:45
  11.9 1.7 fusion.8
  13.6 1.6 broadcast_in_dim.50
  15.2 8.2 %all-to-all-start = ((bf16[8,64,2048]{2,1,0:T(8,128)(2,1)}), bf16[8,64,2048]{2,1,0:T(8,128)(2,1)S(1)}, u32[]{:S(2)}, u32[]{:S(2)}) async-start(bf16[8,64,2048]{2,1,0:T(8,128)(2,1)} %broadcast_in_dim.50), calls=%async_computation | async-start | bytes 4194304 | tf_op jit(solution)/shard_map/all_to_all | solution.py:53
  23.5 1.2 pad_maximum_fusion.1
  24.7 2.8 %collective-permute-start.4 = (bf16[2,2,512,128]{3,2,1,0:T(8,128)(2,1)S(1)}, bf16[2,2,512,128]{3,2,1,0:T(8,128)(2,1)S(1)}, u32[]{:S(2)}, u32[]{:S(2)}) collective-permute-start(bf16[2,2,512,128]{3,2,1,0:T(8,128)(2,1)S(1)} %pad_maximum_fusion.1), channel_id=1, source_target_pairs={{0,48},{16,32},{32,16},{48,0},{1,49},{17,33},{33,17},{49,1},{2,50}... | collective-permute-start | bytes 1572872 | tf_op jit(solution)/shard_map/ppermute | solution.py:45
  27.5 13.5 %collective-permute-done.6.own_x_ref = bf16[1024,640]{1,0:T(8,128)(2,1)} collective-permute-done((bf16[1024,640]{1,0:T(8,128)(2,1)S(1)}, bf16[1024,640]{1,0:T(8,128)(2,1)}, u32[]{:S(2)}, u32[]{:S(2)}) %collective-permute-start.6) | collective-permute-done | bytes 1310752 | tf_op jit(solution)/shard_map/ppermute | solution.py:45
  41.7 1.6 fusion.1.own_ref
  43.8 1.2 pad_maximum_fusion.near_own
  48.4 2.1 %all-to-all-done.x_ref = bf16[8,64,2048]{2,1,0:T(8,128)(2,1)S(1)} async-done(((bf16[8,64,2048]{2,1,0:T(8,128)(2,1)}), bf16[8,64,2048]{2,1,0:T(8,128)(2,1)S(1)}, u32[]{:S(2)}, u32[]{:S(2)}) %all-to-all-start) | async-done | bytes 2097184 | tf_op jit(solution)/shard_map/all_to_all | solution.py:53
  50.5 6.9 %shard_map.118 = bf16[4,128,1408]{2,1,0:T(8,128)(2,1)} custom-call(bf16[8,64,2048]{2,1,0:T(8,128)(2,1)S(1)} %all-to-all-done.x_ref, bf16[1024,640]{1,0:T(8,128)(2,1)S(1)} %fusion.own_ref, bf16[1024,640]{1,0:T(8,128)(2,1)} %collective-permute-done.6.own_x_ref, bf16[1024,640]{1,0:T(8,128)(2,1)} %collective-permute-done.7.peer_ref, ...), custom_call_target="tpu_custom_call" | custom-call | flops 3221225472 | bytes 9437184 | tf_op jit(solution)/shard_map/pallas_call | solution.py:91
  57.4 4.1 %all-to-all-start.1 = ((bf16[4,128,1408]{2,1,0:T(8,128)(2,1)}), bf16[4,128,1408]{2,1,0:T(8,128)(2,1)S(1)}, u32[]{:S(2)}, u32[]{:S(2)}) async-start(bf16[4,128,1408]{2,1,0:T(8,128)(2,1)} %shard_map.118), calls=%async_computation.1 | async-start | bytes 2883584 | tf_op jit(solution)/shard_map/all_to_all | solution.py:53
  61.5 11.8 %collective-permute-done.10.far_own = bf16[4,2,512,128]{3,2,1,0:T(8,128)(2,1)} collective-permute-done((bf16[4,2,512,128]{3,2,1,0:T(8,128)(2,1)}, bf16[4,2,512,128]{3,2,1,0:T(8,128)(2,1)}, u32[]{:S(2)}, u32[]{:S(2)}) %collective-permute-start.10) | collective-permute-done | bytes 1048608 | tf_op jit(solution)/shard_map/ppermute | solution.py:45
  73.9 6.0 %all-to-all-done.1.parts_ref = bf16[4,128,1408]{2,1,0:T(8,128)(2,1)S(1)} async-done(((bf16[4,128,1408]{2,1,0:T(8,128)(2,1)}), bf16[4,128,1408]{2,1,0:T(8,128)(2,1)S(1)}, u32[]{:S(2)}, u32[]{:S(2)}) %all-to-all-start.1) | async-done | bytes 1441824 | tf_op jit(solution)/shard_map/all_to_all | solution.py:53
  79.9 1.1 shard_map.119
  81.1 1.2 collective-permute-done.9
  82.4 1.2 broadcast_in_dim.60
  83.6 3.7 %all-to-all-start.2 = ((bf16[8,2,2,128,128]{4,3,2,1,0:T(8,128)(2,1)}), bf16[8,2,2,128,128]{4,3,2,1,0:T(8,128)(2,1)S(1)}, u32[]{:S(2)}, u32[]{:S(2)}) async-start(bf16[8,2,2,128,128]{4,3,2,1,0:T(8,128)(2,1)} %broadcast_in_dim.60), calls=%async_computation.2 | async-start | bytes 2097152 | tf_op jit(solution)/shard_map/all_to_all | solution.py:53
  87.3 11.0 %shard_map.120 = (f32[1024,256]{1,0:T(8,128)S(1)}, f32[1024,1]{1,0:T(8,128)S(1)}) custom-call(s32[5]{0:T(128)S(1)} %stack.37.place_ref, bf16[1024,128]{1,0:T(8,128)(2,1)S(1)} %bitcast.25, bf16[4,2,512,128]{3,2,1,0:T(8,128)(2,1)} %pad_maximum_fusion.near_own, bf16[4,2,512,128]{3,2,1,0:T(8,128)(2,1)} %collective-permute-done.5.near_peer, ...), custom_call_target="tpu_custom_call" | custom-call | flops 17179869184 | bytes 8388608 | tf_op jit(solution)/shard_map/pallas_call | solution.py:249
  99.3 4.1 %all-to-all-done.2.span_ref = bf16[8,2,2,128,128]{4,3,2,1,0:T(8,128)(2,1)S(1)} async-done(((bf16[8,2,2,128,128]{4,3,2,1,0:T(8,128)(2,1)}), bf16[8,2,2,128,128]{4,3,2,1,0:T(8,128)(2,1)S(1)}, u32[]{:S(2)}, u32[]{:S(2)}) %all-to-all-start.2) | async-done | bytes 1048608 | tf_op jit(solution)/shard_map/all_to_all | solution.py:53
  104.2 1.2 copy-done.2
  105.5 3.9 %shard_map.121 = bf16[128,1024]{1,0:T(8,128)(2,1)S(1)} custom-call(s32[5]{0:T(128)S(1)} %stack.37.place_ref, bf16[1024,128]{1,0:T(8,128)(2,1)S(1)} %bitcast.26, bf16[8,2,2,128,128]{4,3,2,1,0:T(8,128)(2,1)S(1)} %all-to-all-done.2.span_ref, f32[1024,256]{1,0:T(8,128)S(1)} %copy-done.2, f32[1024,1]{1,0:T(8,128)S(1)} %get-tuple-element.48.peak_in), custom_call_target="tpu_custom_call" | custom-call | flops 3221225472 | bytes 4194304 | tf_op jit(solution)/shard_map/pallas_call | solution.py:321
  109.5 17.4 %all_to_all.25.a_ref = bf16[4,128,1024]{2,1,0:T(8,128)(2,1)S(1)} all-to-all(bf16[4,128,1024]{2,1,0:T(8,128)(2,1)S(1)} %broadcast_in_dim.61), channel_id=1, replica_groups={{0,48,64,112},{16,32,80,96},{1,49,65,113},{17,33,81,97},{2,50,66,114},{..., dimensions={0} | all-to-all | bytes 2097152 | tf_op jit(solution)/shard_map/all_to_all | solution.py:53
  126.9 1.5 collective-permute-done.12.own_x_ref
  128.4 2.7 %collective-permute-done.13.peer_x_ref = bf16[512,1024]{1,0:T(8,128)(2,1)S(1)} collective-permute-done((bf16[512,1024]{1,0:T(8,128)(2,1)S(1)}, bf16[512,1024]{1,0:T(8,128)(2,1)S(1)}, u32[]{:S(2)}, u32[]{:S(2)}) %collective-permute-start.13) | collective-permute-done | bytes 1048608 | tf_op jit(solution)/shard_map/ppermute | solution.py:41
  131.1 3.9 %shard_map.122 = bf16[8,64,2048]{2,1,0:T(8,128)(2,1)S(1)} custom-call(bf16[4,128,1024]{2,1,0:T(8,128)(2,1)S(1)} %all_to_all.25.a_ref, bf16[512,1024]{1,0:T(8,128)(2,1)} %fusion.1.own_ref, bf16[512,1024]{1,0:T(8,128)(2,1)} %collective-permute-done.3.peer_ref, bf16[512,1024]{1,0:T(8,128)(2,1)S(1)} %collective-permute-done.12.own_x_ref, ...), custom_call_target="tpu_custom_call" | custom-call | flops 2147483648 | bytes 7340032 | tf_op jit(solution)/shard_map/pallas_call | solution.py:353
  135.0 36.2 %all_to_all.26 = bf16[8,64,2048]{2,1,0:T(8,128)(2,1)S(1)} all-to-all(bf16[8,64,2048]{2,1,0:T(8,128)(2,1)S(1)} %shard_map.122), channel_id=1, replica_groups=mesh['ylo'=2,'x'=4,'z'=4,'yhi'=2,'core'=2] {'z','yhi'}, dimensions={0} | all-to-all | bytes 4194304 | tf_op jit(solution)/shard_map/all_to_all | solution.py:53
  172.1 4.5 %collective-permute-done.14 = bf16[64,1024]{1,0:T(8,128)(2,1)S(1)} collective-permute-done((bf16[64,1024]{1,0:T(8,128)(2,1)S(1)}, bf16[64,1024]{1,0:T(8,128)(2,1)S(1)}, u32[]{:S(2)}, u32[]{:S(2)}) %collective-permute-start.14) | collective-permute-done | bytes 131104 | tf_op jit(solution)/shard_map/ppermute | solution.py:45
  (67 shorter events, 12.2 us)
Async XLA Ops:
  0.0 5.4 %copy-start = (f32[8,16]{1,0:T(8,128)S(1)}, f32[8,16]{1,0:T(8,128)}, u32[]{:S(2)}) copy-start(f32[8,16]{1,0:T(8,128)} %param.18) | copy-start | bytes 1540
  0.0 7.7 %copy-start.4 = (bf16[1024,512]{1,0:T(8,128)(2,1)S(1)}, bf16[1024,512]{1,0:T(8,128)(2,1)}, u32[]{:S(2)}) copy-start(bf16[1024,512]{1,0:T(8,128)(2,1)} %param.14) | copy-start | bytes 3145732
  1.1 8.4 %collective-permute-start = (bf16[64,1024]{1,0:T(8,128)(2,1)S(1)}, bf16[64,1024]{1,0:T(8,128)(2,1)S(1)}, u32[]{:S(2)}, u32[]{:S(2)}) collective-permute-start(bf16[64,1024]{1,0:T(8,128)(2,1)S(1)} %get-tuple-element.56), channel_id=1, source_target_pairs={{0,16},{16,0},{32,48},{48,32},{1,17},{17,1},{33,49},{49,33},{2,18}... | collective-permute-start | bytes 393224 | tf_op jit(solution)/shard_map/ppermute | solution.py:45
  3.7 7.8 %collective-permute-start.1 = (bf16[2,512,128]{2,1,0:T(8,128)(2,1)S(1)}, bf16[2,512,128]{2,1,0:T(8,128)(2,1)S(1)}, u32[]{:S(2)}, u32[]{:S(2)}) collective-permute-start(bf16[2,512,128]{2,1,0:T(8,128)(2,1)S(1)} %constant_dynamic-slice_fusion), channel_id=1, source_target_pairs={{0,64},{64,0},{1,65},{65,1},{2,66},{66,2},{3,67},{67,3},{4,68},{68... | collective-permute-start | bytes 786440 | tf_op jit(solution)/shard_map/ppermute | solution.py:45
  7.7 1.6 copy-start.9
  11.6 3.7 %copy-start.6 = (bf16[2,512,128]{2,1,0:T(8,128)(2,1)}, bf16[2,512,128]{2,1,0:T(8,128)(2,1)S(1)}, u32[]{:S(2)}) copy-start(bf16[2,512,128]{2,1,0:T(8,128)(2,1)S(1)} %collective-permute-done.1) | copy-start | bytes 786436
  11.6 29.4 %collective-permute-start.6 = (bf16[1024,640]{1,0:T(8,128)(2,1)S(1)}, bf16[1024,640]{1,0:T(8,128)(2,1)}, u32[]{:S(2)}, u32[]{:S(2)}) collective-permute-start(bf16[1024,640]{1,0:T(8,128)(2,1)S(1)} %fusion.own_ref), channel_id=1, source_target_pairs={{0,16},{16,0},{32,48},{48,32},{1,17},{17,1},{33,49},{49,33},{2,18}... | collective-permute-start | bytes 3932168 | tf_op jit(solution)/shard_map/ppermute | solution.py:45
  15.2 25.8 %copy-start.10 = (f32[4,8]{1,0:T(4,128)S(1)}, f32[4,8]{1,0:T(4,128)}, u32[]{:S(2)}) copy-start(f32[4,8]{1,0:T(4,128)} %param.21) | copy-start | bytes 388
  15.2 35.2 %all-to-all-start = ((bf16[8,64,2048]{2,1,0:T(8,128)(2,1)}), bf16[8,64,2048]{2,1,0:T(8,128)(2,1)S(1)}, u32[]{:S(2)}, u32[]{:S(2)}) async-start(bf16[8,64,2048]{2,1,0:T(8,128)(2,1)} %broadcast_in_dim.50), calls=%async_computation | async-start | bytes 4194304 | tf_op jit(solution)/shard_map/all_to_all | solution.py:53
  23.5 18.2 %copy-start.5 = (bf16[512,1024]{1,0:T(8,128)(2,1)S(1)}, bf16[512,1024]{1,0:T(8,128)(2,1)}, u32[]{:S(2)}) copy-start(bf16[512,1024]{1,0:T(8,128)(2,1)} %param.20) | copy-start | bytes 3145732
  24.7 19.1 %collective-permute-start.4 = (bf16[2,2,512,128]{3,2,1,0:T(8,128)(2,1)S(1)}, bf16[2,2,512,128]{3,2,1,0:T(8,128)(2,1)S(1)}, u32[]{:S(2)}, u32[]{:S(2)}) collective-permute-start(bf16[2,2,512,128]{3,2,1,0:T(8,128)(2,1)S(1)} %pad_maximum_fusion.1), channel_id=1, source_target_pairs={{0,48},{16,32},{32,16},{48,0},{1,49},{17,33},{33,17},{49,1},{2,50}... | collective-permute-start | bytes 1572872 | tf_op jit(solution)/shard_map/ppermute | solution.py:45
  27.5 23.0 %collective-permute-start.7 = (bf16[1024,640]{1,0:T(8,128)(2,1)S(1)}, bf16[1024,640]{1,0:T(8,128)(2,1)}, u32[]{:S(2)}, u32[]{:S(2)}) collective-permute-start(bf16[1024,640]{1,0:T(8,128)(2,1)S(1)} %fusion.own_ref), channel_id=1, source_target_pairs={{0,1},{1,0},{2,3},{3,2},{4,5},{5,4},{6,7},{7,6},{8,9},{9,8},{10,11... | collective-permute-start | bytes 3932168 | tf_op jit(solution)/shard_map/ppermute | solution.py:41
  41.0 9.4 %collective-permute-start.8 = (bf16[1024,640]{1,0:T(8,128)(2,1)}, bf16[1024,640]{1,0:T(8,128)(2,1)}, u32[]{:S(2)}, u32[]{:S(2)}) collective-permute-start(bf16[1024,640]{1,0:T(8,128)(2,1)} %collective-permute-done.6.own_x_ref), channel_id=1, source_target_pairs={{0,1},{1,0},{2,3},{3,2},{4,5},{5,4},{6,7},{7,6},{8,9},{9,8},{10,11... | collective-permute-start | bytes 3932168 | tf_op jit(solution)/shard_map/ppermute | solution.py:41
  41.6 2.1 %copy-start.3 = (bf16[1,2,512,128]{3,2,1,0:T(8,128)(2,1)S(1)}, bf16[1,2,512,128]{3,2,1,0:T(8,128)(2,1)}, u32[]{:S(2)}) copy-start(bf16[1,2,512,128]{3,2,1,0:T(8,128)(2,1)} %fusion.8) | copy-start | bytes 786436
  41.7 2.1 %copy-start.7 = (bf16[2,512,128]{2,1,0:T(8,128)(2,1)S(1)}, bf16[2,512,128]{2,1,0:T(8,128)(2,1)}, u32[]{:S(2)}) copy-start(bf16[2,512,128]{2,1,0:T(8,128)(2,1)} %copy-done.6) | copy-start | bytes 786436
  43.3 2.5 %copy-start.8 = (f32[512]{0:T(512)S(1)}, f32[512]{0:T(512)}, u32[]{:S(2)}) copy-start(f32[512]{0:T(512)} %param.16) | copy-start | bytes 6148
  43.3 5.1 %collective-permute-start.3 = (bf16[512,1024]{1,0:T(8,128)(2,1)}, bf16[512,1024]{1,0:T(8,128)(2,1)}, u32[]{:S(2)}, u32[]{:S(2)}) collective-permute-start(bf16[512,1024]{1,0:T(8,128)(2,1)} %fusion.1.own_ref), channel_id=1, source_target_pairs={{0,1},{1,0},{2,3},{3,2},{4,5},{5,4},{6,7},{7,6},{8,9},{9,8},{10,11... | collective-permute-start | bytes 3145736 | tf_op jit(solution)/shard_map/ppermute | solution.py:41
  44.9 3.4 %collective-permute-start.5 = (bf16[4,2,512,128]{3,2,1,0:T(8,128)(2,1)}, bf16[4,2,512,128]{3,2,1,0:T(8,128)(2,1)}, u32[]{:S(2)}, u32[]{:S(2)}) collective-permute-start(bf16[4,2,512,128]{3,2,1,0:T(8,128)(2,1)} %pad_maximum_fusion.near_own), channel_id=1, source_target_pairs={{0,1},{1,0},{2,3},{3,2},{4,5},{5,4},{6,7},{7,6},{8,9},{9,8},{10,11... | collective-permute-start | bytes 3145736 | tf_op jit(solution)/shard_map/ppermute | solution.py:41
  45.7 1.9 %collective-permute-start.2 = (f32[640]{0:T(1024)S(1)}, f32[640]{0:T(1024)S(1)}, u32[]{:S(2)}, u32[]{:S(2)}) collective-permute-start(f32[640]{0:T(1024)S(1)} %pad_maximum_fusion.6), channel_id=1, source_target_pairs={{0,1},{1,0},{2,3},{3,2},{4,5},{5,4},{6,7},{7,6},{8,9},{9,8},{10,11... | collective-permute-start | bytes 7688 | tf_op jit(solution)/shard_map/ppermute | solution.py:41
  47.6 25.7 %collective-permute-start.10 = (bf16[4,2,512,128]{3,2,1,0:T(8,128)(2,1)}, bf16[4,2,512,128]{3,2,1,0:T(8,128)(2,1)}, u32[]{:S(2)}, u32[]{:S(2)}) collective-permute-start(bf16[4,2,512,128]{3,2,1,0:T(8,128)(2,1)} %pad_maximum_fusion.near_own), channel_id=1, source_target_pairs={{0,16},{16,0},{32,48},{48,32},{1,17},{17,1},{33,49},{49,33},{2,18}... | collective-permute-start | bytes 3145736 | tf_op jit(solution)/shard_map/ppermute | solution.py:45
  57.4 22.5 %all-to-all-start.1 = ((bf16[4,128,1408]{2,1,0:T(8,128)(2,1)}), bf16[4,128,1408]{2,1,0:T(8,128)(2,1)S(1)}, u32[]{:S(2)}, u32[]{:S(2)}) async-start(bf16[4,128,1408]{2,1,0:T(8,128)(2,1)} %shard_map.118), calls=%async_computation.1 | async-start | bytes 2883584 | tf_op jit(solution)/shard_map/all_to_all | solution.py:53
  73.3 14.0 %collective-permute-start.11 = (bf16[4,2,512,128]{3,2,1,0:T(8,128)(2,1)}, bf16[4,2,512,128]{3,2,1,0:T(8,128)(2,1)S(1)}, u32[]{:S(2)}, u32[]{:S(2)}) collective-permute-start(bf16[4,2,512,128]{3,2,1,0:T(8,128)(2,1)} %collective-permute-done.10.far_own), channel_id=1, source_target_pairs={{0,1},{1,0},{2,3},{3,2},{4,5},{5,4},{6,7},{7,6},{8,9},{9,8},{10,11... | collective-permute-start | bytes 3145736 | tf_op jit(solution)/shard_map/ppermute | solution.py:41
  81.0 1.3 collective-permute-start.9
  83.6 19.8 %all-to-all-start.2 = ((bf16[8,2,2,128,128]{4,3,2,1,0:T(8,128)(2,1)}), bf16[8,2,2,128,128]{4,3,2,1,0:T(8,128)(2,1)S(1)}, u32[]{:S(2)}, u32[]{:S(2)}) async-start(bf16[8,2,2,128,128]{4,3,2,1,0:T(8,128)(2,1)} %broadcast_in_dim.60), calls=%async_computation.2 | async-start | bytes 2097152 | tf_op jit(solution)/shard_map/all_to_all | solution.py:53
  98.4 1.0 copy-start.1
  103.4 25.0 %collective-permute-start.12 = (bf16[512,1024]{1,0:T(8,128)(2,1)}, bf16[512,1024]{1,0:T(8,128)(2,1)S(1)}, u32[]{:S(2)}, u32[]{:S(2)}) collective-permute-start(bf16[512,1024]{1,0:T(8,128)(2,1)} %fusion.1.own_ref), channel_id=1, source_target_pairs={{0,16},{16,0},{32,48},{48,32},{1,17},{17,1},{33,49},{49,33},{2,18}... | collective-permute-start | bytes 3145736 | tf_op jit(solution)/shard_map/ppermute | solution.py:45
  104.2 1.2 copy-start.2
  128.4 2.7 %collective-permute-start.13 = (bf16[512,1024]{1,0:T(8,128)(2,1)S(1)}, bf16[512,1024]{1,0:T(8,128)(2,1)S(1)}, u32[]{:S(2)}, u32[]{:S(2)}) collective-permute-start(bf16[512,1024]{1,0:T(8,128)(2,1)S(1)} %collective-permute-done.12.own_x_ref), channel_id=1, source_target_pairs={{0,1},{1,0},{2,3},{3,2},{4,5},{5,4},{6,7},{7,6},{8,9},{9,8},{10,11... | collective-permute-start | bytes 3145736 | tf_op jit(solution)/shard_map/ppermute | solution.py:41
  171.6 5.0 %collective-permute-start.14 = (bf16[64,1024]{1,0:T(8,128)(2,1)S(1)}, bf16[64,1024]{1,0:T(8,128)(2,1)S(1)}, u32[]{:S(2)}, u32[]{:S(2)}) collective-permute-start(bf16[64,1024]{1,0:T(8,128)(2,1)S(1)} %get-tuple-element.54), channel_id=1, source_target_pairs={{0,16},{16,0},{32,48},{48,32},{1,17},{17,1},{33,49},{49,33},{2,18}... | collective-permute-start | bytes 393224 | tf_op jit(solution)/shard_map/ppermute | solution.py:45

commit v4 on v3

--- a/solution.py
+++ b/solution.py
@@ -30,6 +30,7 @@
 NEAR = (0, 4, 3, 7)
 FAR = (1, 5, 2, 6)
 MEMBERS = ((0, 3, 4, 7), (1, 2, 5, 6))
+PAIRS = (tuple(range(16)), tuple(range(16, 32)))
 VMEM = 26 * 2**20
 
 
@@ -336,30 +337,38 @@
     )(place, queries, span, acc, peak)
 
 
-def mix_kernel(a_ref, own_ref, peer_ref, own_x_ref, peer_x_ref, out_ref):
+def mix_kernel(side_ref, a_ref, own_ref, peer_ref, own_x_ref, peer_x_ref, out_ref):
     a = a_ref[...].reshape(4 * TOK, GROUP * HD)
     width = 4 * HD
-    for start, near, far in ((0, own_ref, peer_ref), (SLOTS, own_x_ref, peer_x_ref)):
-        total = jnp.dot(a[:, :width], near[...], preferred_element_type=jnp.float32)
-        total = total + jnp.dot(a[:, width:], far[...], preferred_element_type=jnp.float32)
-        total = total.astype(jnp.bfloat16)
-        for block in range(GROUP):
-            member, row = place_of(block)
-            row = row + member * TOK
-            out_ref[block, :, start : start + SLOTS] = total[row : row + PART]
-
-
-def mix(attended, *weights):
+
+    def fill(side):
+        for to, near, far in ((side, own_ref, peer_ref), (1 - side, own_x_ref, peer_x_ref)):
+            total = jnp.dot(a[:, :width], near[...], preferred_element_type=jnp.float32)
+            total = total + jnp.dot(a[:, width:], far[...], preferred_element_type=jnp.float32)
+            total = total.astype(jnp.bfloat16)
+            for block in range(GROUP):
+                member, row = place_of(block)
+                row = row + member * TOK
+                out_ref[to, block] = total[row : row + PART]
+
+    for side in range(2):
+
+        @pl.when(side_ref[0] == side)
+        def _(side=side):
+            fill(side)
+
+
+def mix(side, attended, *weights):
     return pl.pallas_call(
         mix_kernel,
-        out_shape=jax.ShapeDtypeStruct((GROUP, PART, 2 * SLOTS), jnp.bfloat16),
-        in_specs=in_vmem(5),
+        out_shape=jax.ShapeDtypeStruct((2, GROUP, PART, SLOTS), jnp.bfloat16),
+        in_specs=[pl.BlockSpec(memory_space=pltpu.SMEM)] + in_vmem(5),
         out_specs=pl.BlockSpec(memory_space=pltpu.VMEM),
         compiler_params=pltpu.CompilerParams(vmem_limit_bytes=VMEM),
         cost_estimate=pl.CostEstimate(
             flops=2 * 2**30, bytes_accessed=7 * 2**20, transcendentals=0
         ),
-    )(attended, *weights)
+    )(side, attended, *weights)
 
 
 def body(
@@ -439,21 +448,19 @@
     queries, pair_kv = tie((queries, copies(pair_kv, GROUP)))
     span = exchange(pair_kv, ROW)
     state = attend_cache(place, queries, near, near_peer, far, swap_cores(far))
-    state, span, out_own = tie((state, span, out_own))
+    state, out_own = tie((state, out_own))
     out_own_x = beside(out_own)
     attended = attend_span(place, queries, span, *state)
 
     everyone = exchange(copies(attended, 4), ROW, MEMBERS)
     everyone, out_own_x = tie((everyone, out_own_x))
     out_peer_x = swap_cores(out_own_x)
-    mixed = mix(everyone, out_own, out_peer, out_own_x, out_peer_x)
-    shares = exchange(mixed, COL)
-    total = jnp.sum(shares.astype(jnp.float32), axis=0).astype(jnp.bfloat16)
-    mine = total[:, :SLOTS]
-    other = beside(total[:, SLOTS:])
-    return jnp.where(
-        half == 0, jnp.concatenate([mine, other]), jnp.concatenate([other, mine])
-    )
+    side = jnp.reshape(x & 1, (1,)).astype(jnp.int32)
+    mixed = mix(side, everyone, out_own, out_peer, out_own_x, out_peer_x)
+    shares = exchange(mixed.reshape(2 * GROUP, PART, SLOTS), ("x",) + COL, PAIRS)
+    shares = shares.reshape(2, GROUP, PART, SLOTS).astype(jnp.float32)
+    total = jnp.sum(shares, axis=1).astype(jnp.bfloat16)
+    return jnp.where(x < 2, total, total[::-1]).reshape(TOK, SLOTS)
 
 
 def solution(mesh):

time: 178 us -> 177 us (level)
  blocking collectives: 53.5 us -> 0 us
  waiting for transfers between devices: 50 us -> 86.9 us
  starting transfers between devices: 25.5 us -> 37.1 us
    all_to_all x2 -> x0, blocking collectives: 53.5 us -> none  [exchange(): lax.all_to_all(array, axes, 0, 0, tiled=True, axis_index_groups=groups)]
    all_to_all x3 -> x5, waiting for transfers between devices: 12.1 us -> 43.5 us  [exchange(): lax.all_to_all(array, axes, 0, 0, tiled=True, axis_index_groups=groups)]
    all_to_all x3 -> x5, starting transfers between devices: 16.1 us -> 27.4 us  [exchange(): lax.all_to_all(array, axes, 0, 0, tiled=True, axis_index_groups=groups)]
    ppermute x7 -> x6, waiting for transfers between devices: 33.4 us -> 38.9 us  [along(): return lax.ppermute(array, axis, [(i, i ^ distance) for i in range(size)])]
    ppermute x7 -> x6, starting transfers between devices: 8.16 us -> 8.53 us  [along(): return lax.ppermute(array, axis, [(i, i ^ distance) for i in range(size)])]
  transfers between devices with their start and end apart: 18 -> 19, of which waited for: 11 -> 12; matrix products, arithmetic and copies ran while one was open for 9% -> 10% of each run, Pallas kernels for 13% -> 13%
where the time goes in v4:
time: 177 us; the launch traced here: 175 us
  waiting for transfers between devices  86.9 us (49%)
  starting transfers between devices  37.1 us (21%)
  Pallas kernels  28.3 us (16%)
  local copies, waits for them, and re-layouts  14.2 us (8%)
  other arithmetic  7.21 us (4%)
    all_to_all x5, waiting for transfers between devices, exchange(): lax.all_to_all(array, axes, 0, 0, tiled=True, axis_index_groups=groups)  43.5 us
    ppermute x6, waiting for transfers between devices, along(): return lax.ppermute(array, axis, [(i, i ^ distance) for i in range(size)])  38.9 us
    all_to_all x5, starting transfers between devices, exchange(): lax.all_to_all(array, axes, 0, 0, tiled=True, axis_index_groups=groups)  27.4 us
    pallas_call x1, Pallas kernels, attend_cache(): pl.pallas_call(cache_kernel, out_shape=(jax.ShapeDtypeStruct((ROWS, 2 * H...  11 us
    ppermute x6, starting transfers between devices, along(): return lax.ppermute(array, axis, [(i, i ^ distance) for i in range(size)])  8.53 us
    pallas_call x1, Pallas kernels, project(): pl.pallas_call(project_kernel, out_shape=jax.ShapeDtypeStruct((4, TOK, SQ...  6.95 us
    pallas_call x1, Pallas kernels, mix(): pl.pallas_call(mix_kernel, out_shape=jax.ShapeDtypeStruct((2, GROUP, PART...  5.31 us
    ppermute x8, waiting for transfers between devices, swap_cores(): return lax.ppermute(array, 'core', [(0, 1), (1, 0)])  4.46 us
  transfers between devices with their start and end apart: 19, of which 12 were waited for; matrix products, arithmetic and copies ran while one was open for 10% of the time, Pallas kernels for 13%

profile of v4, /device:TPU:0, one launch (start us, length us, event | category | flops | bytes accessed | tf_op | source)
XLA Modules:
  0.0 174.7 jit_solution(13931482900791633724)
XLA Ops:
  1.1 1.7 collective-permute-start
  3.7 1.7 collective-permute-start.1
  6.4 1.2 broadcast_in_dim.57
  9.5 2.0 %collective-permute-done.1 = bf16[2,512,128]{2,1,0:T(8,128)(2,1)S(1)} collective-permute-done((bf16[2,512,128]{2,1,0:T(8,128)(2,1)S(1)}, bf16[2,512,128]{2,1,0:T(8,128)(2,1)S(1)}, u32[]{:S(2)}, u32[]{:S(2)}) %collective-permute-start.1) | collective-permute-done | bytes 262176 | tf_op jit(solution)/shard_map/ppermute | solution.py:46
  11.9 1.7 fusion.7
  13.6 1.6 broadcast_in_dim.50
  15.2 8.2 %all-to-all-start = ((bf16[8,64,2048]{2,1,0:T(8,128)(2,1)}), bf16[8,64,2048]{2,1,0:T(8,128)(2,1)S(1)}, u32[]{:S(2)}, u32[]{:S(2)}) async-start(bf16[8,64,2048]{2,1,0:T(8,128)(2,1)} %broadcast_in_dim.50), calls=%async_computation | async-start | bytes 4194304 | tf_op jit(solution)/shard_map/all_to_all | solution.py:54
  23.5 1.2 pad_maximum_fusion.1
  24.7 2.8 %collective-permute-start.4 = (bf16[2,2,512,128]{3,2,1,0:T(8,128)(2,1)S(1)}, bf16[2,2,512,128]{3,2,1,0:T(8,128)(2,1)S(1)}, u32[]{:S(2)}, u32[]{:S(2)}) collective-permute-start(bf16[2,2,512,128]{3,2,1,0:T(8,128)(2,1)S(1)} %pad_maximum_fusion.1), channel_id=1, source_target_pairs={{0,48},{16,32},{32,16},{48,0},{1,49},{17,33},{33,17},{49,1},{2,50}... | collective-permute-start | bytes 1572872 | tf_op jit(solution)/shard_map/ppermute | solution.py:46
  27.5 13.5 %collective-permute-done.6.own_x_ref = bf16[1024,640]{1,0:T(8,128)(2,1)} collective-permute-done((bf16[1024,640]{1,0:T(8,128)(2,1)S(1)}, bf16[1024,640]{1,0:T(8,128)(2,1)}, u32[]{:S(2)}, u32[]{:S(2)}) %collective-permute-start.6) | collective-permute-done | bytes 1310752 | tf_op jit(solution)/shard_map/ppermute | solution.py:46
  41.7 1.6 fusion.1.own_ref
  43.8 1.2 pad_maximum_fusion.near_own
  48.3 2.1 %all-to-all-done.x_ref = bf16[8,64,2048]{2,1,0:T(8,128)(2,1)S(1)} async-done(((bf16[8,64,2048]{2,1,0:T(8,128)(2,1)}), bf16[8,64,2048]{2,1,0:T(8,128)(2,1)S(1)}, u32[]{:S(2)}, u32[]{:S(2)}) %all-to-all-start) | async-done | bytes 2097184 | tf_op jit(solution)/shard_map/all_to_all | solution.py:54
  50.5 6.9 %shard_map.118 = bf16[4,128,1408]{2,1,0:T(8,128)(2,1)} custom-call(bf16[8,64,2048]{2,1,0:T(8,128)(2,1)S(1)} %all-to-all-done.x_ref, bf16[1024,640]{1,0:T(8,128)(2,1)S(1)} %fusion.own_ref, bf16[1024,640]{1,0:T(8,128)(2,1)} %collective-permute-done.6.own_x_ref, bf16[1024,640]{1,0:T(8,128)(2,1)} %collective-permute-done.7.peer_ref, ...), custom_call_target="tpu_custom_call" | custom-call | flops 3221225472 | bytes 9437184 | tf_op jit(solution)/shard_map/pallas_call | solution.py:92
  57.4 4.1 %all-to-all-start.1 = ((bf16[4,128,1408]{2,1,0:T(8,128)(2,1)}), bf16[4,128,1408]{2,1,0:T(8,128)(2,1)S(1)}, u32[]{:S(2)}, u32[]{:S(2)}) async-start(bf16[4,128,1408]{2,1,0:T(8,128)(2,1)} %shard_map.118), calls=%async_computation.1 | async-start | bytes 2883584 | tf_op jit(solution)/shard_map/all_to_all | solution.py:54
  61.5 11.8 %collective-permute-done.10.far_own = bf16[4,2,512,128]{3,2,1,0:T(8,128)(2,1)} collective-permute-done((bf16[4,2,512,128]{3,2,1,0:T(8,128)(2,1)}, bf16[4,2,512,128]{3,2,1,0:T(8,128)(2,1)}, u32[]{:S(2)}, u32[]{:S(2)}) %collective-permute-start.10) | collective-permute-done | bytes 1048608 | tf_op jit(solution)/shard_map/ppermute | solution.py:46
  73.9 6.0 %all-to-all-done.1.parts_ref = bf16[4,128,1408]{2,1,0:T(8,128)(2,1)S(1)} async-done(((bf16[4,128,1408]{2,1,0:T(8,128)(2,1)}), bf16[4,128,1408]{2,1,0:T(8,128)(2,1)S(1)}, u32[]{:S(2)}, u32[]{:S(2)}) %all-to-all-start.1) | async-done | bytes 1441824 | tf_op jit(solution)/shard_map/all_to_all | solution.py:54
  81.1 1.2 collective-permute-done.9
  82.4 1.2 broadcast_in_dim.60
  83.6 3.7 %all-to-all-start.2 = ((bf16[8,2,2,128,128]{4,3,2,1,0:T(8,128)(2,1)}), bf16[8,2,2,128,128]{4,3,2,1,0:T(8,128)(2,1)S(1)}, u32[]{:S(2)}, u32[]{:S(2)}) async-start(bf16[8,2,2,128,128]{4,3,2,1,0:T(8,128)(2,1)} %broadcast_in_dim.60), calls=%async_computation.2 | async-start | bytes 2097152 | tf_op jit(solution)/shard_map/all_to_all | solution.py:54
  87.3 11.0 %shard_map.120 = (f32[1024,256]{1,0:T(8,128)S(1)}, f32[1024,1]{1,0:T(8,128)S(1)}) custom-call(s32[5]{0:T(128)S(1)} %stack.37.place_ref, bf16[1024,128]{1,0:T(8,128)(2,1)S(1)} %bitcast.30, bf16[4,2,512,128]{3,2,1,0:T(8,128)(2,1)} %pad_maximum_fusion.near_own, bf16[4,2,512,128]{3,2,1,0:T(8,128)(2,1)} %collective-permute-done.5.near_peer, ...), custom_call_target="tpu_custom_call" | custom-call | flops 17179869184 | bytes 8388608 | tf_op jit(solution)/shard_map/pallas_call | solution.py:250
  99.3 1.7 collective-permute-start.12
  101.1 2.3 %all-to-all-done.2.span_ref = bf16[8,2,2,128,128]{4,3,2,1,0:T(8,128)(2,1)S(1)} async-done(((bf16[8,2,2,128,128]{4,3,2,1,0:T(8,128)(2,1)}), bf16[8,2,2,128,128]{4,3,2,1,0:T(8,128)(2,1)S(1)}, u32[]{:S(2)}, u32[]{:S(2)}) %all-to-all-start.2) | async-done | bytes 1048608 | tf_op jit(solution)/shard_map/all_to_all | solution.py:54
  103.4 1.2 copy-done.2
  104.6 3.9 %shard_map.121 = bf16[128,1024]{1,0:T(8,128)(2,1)S(1)} custom-call(s32[5]{0:T(128)S(1)} %stack.37.place_ref, bf16[1024,128]{1,0:T(8,128)(2,1)S(1)} %bitcast.31, bf16[8,2,2,128,128]{4,3,2,1,0:T(8,128)(2,1)S(1)} %all-to-all-done.2.span_ref, f32[1024,256]{1,0:T(8,128)S(1)} %copy-done.2, f32[1024,1]{1,0:T(8,128)S(1)} %get-tuple-element.46.peak_in), custom_call_target="tpu_custom_call" | custom-call | flops 3221225472 | bytes 4194304 | tf_op jit(solution)/shard_map/pallas_call | solution.py:322
  109.6 3.5 %all-to-all-start.3 = ((bf16[4,128,1024]{2,1,0:T(8,128)(2,1)}), bf16[4,128,1024]{2,1,0:T(8,128)(2,1)S(1)}, u32[]{:S(2)}, u32[]{:S(2)}) async-start(bf16[4,128,1024]{2,1,0:T(8,128)(2,1)} %broadcast_in_dim.61), calls=%async_computation.3 | async-start | bytes 2097152 | tf_op jit(solution)/shard_map/all_to_all | solution.py:54
  113.1 11.6 %collective-permute-done.12.own_x_ref = bf16[512,1024]{1,0:T(8,128)(2,1)S(1)} collective-permute-done((bf16[512,1024]{1,0:T(8,128)(2,1)}, bf16[512,1024]{1,0:T(8,128)(2,1)S(1)}, u32[]{:S(2)}, u32[]{:S(2)}) %collective-permute-start.12) | collective-permute-done | bytes 1048608 | tf_op jit(solution)/shard_map/ppermute | solution.py:46
  124.8 3.4 %all-to-all-done.3.a_ref = bf16[4,128,1024]{2,1,0:T(8,128)(2,1)S(1)} async-done(((bf16[4,128,1024]{2,1,0:T(8,128)(2,1)}), bf16[4,128,1024]{2,1,0:T(8,128)(2,1)S(1)}, u32[]{:S(2)}, u32[]{:S(2)}) %all-to-all-start.3) | async-done | bytes 1048608 | tf_op jit(solution)/shard_map/all_to_all | solution.py:54
  128.2 2.7 %collective-permute-done.13.peer_x_ref = bf16[512,1024]{1,0:T(8,128)(2,1)S(1)} collective-permute-done((bf16[512,1024]{1,0:T(8,128)(2,1)S(1)}, bf16[512,1024]{1,0:T(8,128)(2,1)S(1)}, u32[]{:S(2)}, u32[]{:S(2)}) %collective-permute-start.13) | collective-permute-done | bytes 1048608 | tf_op jit(solution)/shard_map/ppermute | solution.py:42
  130.8 5.3 %shard_map.122 = bf16[2,8,64,1024]{3,2,1,0:T(8,128)(2,1)} custom-call(s32[1]{0:T(128)} %bitcast.side_ref, bf16[4,128,1024]{2,1,0:T(8,128)(2,1)S(1)} %all-to-all-done.3.a_ref, bf16[512,1024]{1,0:T(8,128)(2,1)} %fusion.1.own_ref, bf16[512,1024]{1,0:T(8,128)(2,1)} %collective-permute-done.3.peer_ref, bf16[512,1024]{1,0:T(8,128)(2,1)S(1)} %collective-permute-done.12.own_x_ref, ...), custom_call_target="tpu_custom_call" | custom-call | flops 2147483648 | bytes 7340032 | tf_op jit(solution)/shard_map/pallas_call | solution.py:362
  136.1 7.8 %all-to-all-start.4 = ((bf16[16,64,1024]{2,1,0:T(8,128)(2,1)}), bf16[16,64,1024]{2,1,0:T(8,128)(2,1)S(1)}, u32[]{:S(2)}, u32[]{:S(2)}) async-start(bf16[16,64,1024]{2,1,0:T(8,128)(2,1)} %bitcast.14), calls=%async_computation.4 | async-start | bytes 4194304 | tf_op jit(solution)/shard_map/all_to_all | solution.py:54
  143.9 29.7 %all-to-all-done.4 = bf16[16,64,1024]{2,1,0:T(8,128)(2,1)S(1)} async-done(((bf16[16,64,1024]{2,1,0:T(8,128)(2,1)}), bf16[16,64,1024]{2,1,0:T(8,128)(2,1)S(1)}, u32[]{:S(2)}, u32[]{:S(2)}) %all-to-all-start.4) | async-done | bytes 2097184 | tf_op jit(solution)/shard_map/all_to_all | solution.py:54
  (66 shorter events, 14.1 us)
Async XLA Ops:
  0.0 5.4 %copy-start = (f32[8,16]{1,0:T(8,128)S(1)}, f32[8,16]{1,0:T(8,128)}, u32[]{:S(2)}) copy-start(f32[8,16]{1,0:T(8,128)} %param.18) | copy-start | bytes 1540
  0.0 7.7 %copy-start.4 = (bf16[1024,512]{1,0:T(8,128)(2,1)S(1)}, bf16[1024,512]{1,0:T(8,128)(2,1)}, u32[]{:S(2)}) copy-start(bf16[1024,512]{1,0:T(8,128)(2,1)} %param.14) | copy-start | bytes 3145732
  1.1 8.4 %collective-permute-start = (bf16[64,1024]{1,0:T(8,128)(2,1)S(1)}, bf16[64,1024]{1,0:T(8,128)(2,1)S(1)}, u32[]{:S(2)}, u32[]{:S(2)}) collective-permute-start(bf16[64,1024]{1,0:T(8,128)(2,1)S(1)} %get-tuple-element.52), channel_id=1, source_target_pairs={{0,16},{16,0},{32,48},{48,32},{1,17},{17,1},{33,49},{49,33},{2,18}... | collective-permute-start | bytes 393224 | tf_op jit(solution)/shard_map/ppermute | solution.py:46
  3.7 7.8 %collective-permute-start.1 = (bf16[2,512,128]{2,1,0:T(8,128)(2,1)S(1)}, bf16[2,512,128]{2,1,0:T(8,128)(2,1)S(1)}, u32[]{:S(2)}, u32[]{:S(2)}) collective-permute-start(bf16[2,512,128]{2,1,0:T(8,128)(2,1)S(1)} %constant_dynamic-slice_fusion), channel_id=1, source_target_pairs={{0,64},{64,0},{1,65},{65,1},{2,66},{66,2},{3,67},{67,3},{4,68},{68... | collective-permute-start | bytes 786440 | tf_op jit(solution)/shard_map/ppermute | solution.py:46
  7.7 1.6 copy-start.9
  11.6 3.7 %copy-start.6 = (bf16[2,512,128]{2,1,0:T(8,128)(2,1)}, bf16[2,512,128]{2,1,0:T(8,128)(2,1)S(1)}, u32[]{:S(2)}) copy-start(bf16[2,512,128]{2,1,0:T(8,128)(2,1)S(1)} %collective-permute-done.1) | copy-start | bytes 786436
  11.6 29.4 %collective-permute-start.6 = (bf16[1024,640]{1,0:T(8,128)(2,1)S(1)}, bf16[1024,640]{1,0:T(8,128)(2,1)}, u32[]{:S(2)}, u32[]{:S(2)}) collective-permute-start(bf16[1024,640]{1,0:T(8,128)(2,1)S(1)} %fusion.own_ref), channel_id=1, source_target_pairs={{0,16},{16,0},{32,48},{48,32},{1,17},{17,1},{33,49},{49,33},{2,18}... | collective-permute-start | bytes 3932168 | tf_op jit(solution)/shard_map/ppermute | solution.py:46
  15.2 25.8 %copy-start.10 = (f32[4,8]{1,0:T(4,128)S(1)}, f32[4,8]{1,0:T(4,128)}, u32[]{:S(2)}) copy-start(f32[4,8]{1,0:T(4,128)} %param.21) | copy-start | bytes 388
  15.2 35.2 %all-to-all-start = ((bf16[8,64,2048]{2,1,0:T(8,128)(2,1)}), bf16[8,64,2048]{2,1,0:T(8,128)(2,1)S(1)}, u32[]{:S(2)}, u32[]{:S(2)}) async-start(bf16[8,64,2048]{2,1,0:T(8,128)(2,1)} %broadcast_in_dim.50), calls=%async_computation | async-start | bytes 4194304 | tf_op jit(solution)/shard_map/all_to_all | solution.py:54
  23.5 18.2 %copy-start.5 = (bf16[512,1024]{1,0:T(8,128)(2,1)S(1)}, bf16[512,1024]{1,0:T(8,128)(2,1)}, u32[]{:S(2)}) copy-start(bf16[512,1024]{1,0:T(8,128)(2,1)} %param.20) | copy-start | bytes 3145732
  24.7 19.1 %collective-permute-start.4 = (bf16[2,2,512,128]{3,2,1,0:T(8,128)(2,1)S(1)}, bf16[2,2,512,128]{3,2,1,0:T(8,128)(2,1)S(1)}, u32[]{:S(2)}, u32[]{:S(2)}) collective-permute-start(bf16[2,2,512,128]{3,2,1,0:T(8,128)(2,1)S(1)} %pad_maximum_fusion.1), channel_id=1, source_target_pairs={{0,48},{16,32},{32,16},{48,0},{1,49},{17,33},{33,17},{49,1},{2,50}... | collective-permute-start | bytes 1572872 | tf_op jit(solution)/shard_map/ppermute | solution.py:46
  27.5 23.0 %collective-permute-start.7 = (bf16[1024,640]{1,0:T(8,128)(2,1)S(1)}, bf16[1024,640]{1,0:T(8,128)(2,1)}, u32[]{:S(2)}, u32[]{:S(2)}) collective-permute-start(bf16[1024,640]{1,0:T(8,128)(2,1)S(1)} %fusion.own_ref), channel_id=1, source_target_pairs={{0,1},{1,0},{2,3},{3,2},{4,5},{5,4},{6,7},{7,6},{8,9},{9,8},{10,11... | collective-permute-start | bytes 3932168 | tf_op jit(solution)/shard_map/ppermute | solution.py:42
  41.0 9.5 %collective-permute-start.8 = (bf16[1024,640]{1,0:T(8,128)(2,1)}, bf16[1024,640]{1,0:T(8,128)(2,1)}, u32[]{:S(2)}, u32[]{:S(2)}) collective-permute-start(bf16[1024,640]{1,0:T(8,128)(2,1)} %collective-permute-done.6.own_x_ref), channel_id=1, source_target_pairs={{0,1},{1,0},{2,3},{3,2},{4,5},{5,4},{6,7},{7,6},{8,9},{9,8},{10,11... | collective-permute-start | bytes 3932168 | tf_op jit(solution)/shard_map/ppermute | solution.py:42
  41.6 2.1 %copy-start.3 = (bf16[1,2,512,128]{3,2,1,0:T(8,128)(2,1)S(1)}, bf16[1,2,512,128]{3,2,1,0:T(8,128)(2,1)}, u32[]{:S(2)}) copy-start(bf16[1,2,512,128]{3,2,1,0:T(8,128)(2,1)} %fusion.7) | copy-start | bytes 786436
  41.7 2.1 %copy-start.7 = (bf16[2,512,128]{2,1,0:T(8,128)(2,1)S(1)}, bf16[2,512,128]{2,1,0:T(8,128)(2,1)}, u32[]{:S(2)}) copy-start(bf16[2,512,128]{2,1,0:T(8,128)(2,1)} %copy-done.6) | copy-start | bytes 786436
  43.2 2.5 %copy-start.8 = (f32[512]{0:T(512)S(1)}, f32[512]{0:T(512)}, u32[]{:S(2)}) copy-start(f32[512]{0:T(512)} %param.16) | copy-start | bytes 6148
  43.2 5.1 %collective-permute-start.3 = (bf16[512,1024]{1,0:T(8,128)(2,1)}, bf16[512,1024]{1,0:T(8,128)(2,1)}, u32[]{:S(2)}, u32[]{:S(2)}) collective-permute-start(bf16[512,1024]{1,0:T(8,128)(2,1)} %fusion.1.own_ref), channel_id=1, source_target_pairs={{0,1},{1,0},{2,3},{3,2},{4,5},{5,4},{6,7},{7,6},{8,9},{9,8},{10,11... | collective-permute-start | bytes 3145736 | tf_op jit(solution)/shard_map/ppermute | solution.py:42
  44.9 3.4 %collective-permute-start.5 = (bf16[4,2,512,128]{3,2,1,0:T(8,128)(2,1)}, bf16[4,2,512,128]{3,2,1,0:T(8,128)(2,1)}, u32[]{:S(2)}, u32[]{:S(2)}) collective-permute-start(bf16[4,2,512,128]{3,2,1,0:T(8,128)(2,1)} %pad_maximum_fusion.near_own), channel_id=1, source_target_pairs={{0,1},{1,0},{2,3},{3,2},{4,5},{5,4},{6,7},{7,6},{8,9},{9,8},{10,11... | collective-permute-start | bytes 3145736 | tf_op jit(solution)/shard_map/ppermute | solution.py:42
  45.7 1.9 %collective-permute-start.2 = (f32[640]{0:T(1024)S(1)}, f32[640]{0:T(1024)S(1)}, u32[]{:S(2)}, u32[]{:S(2)}) collective-permute-start(f32[640]{0:T(1024)S(1)} %pad_maximum_fusion.6), channel_id=1, source_target_pairs={{0,1},{1,0},{2,3},{3,2},{4,5},{5,4},{6,7},{7,6},{8,9},{9,8},{10,11... | collective-permute-start | bytes 7688 | tf_op jit(solution)/shard_map/ppermute | solution.py:42
  47.6 25.7 %collective-permute-start.10 = (bf16[4,2,512,128]{3,2,1,0:T(8,128)(2,1)}, bf16[4,2,512,128]{3,2,1,0:T(8,128)(2,1)}, u32[]{:S(2)}, u32[]{:S(2)}) collective-permute-start(bf16[4,2,512,128]{3,2,1,0:T(8,128)(2,1)} %pad_maximum_fusion.near_own), channel_id=1, source_target_pairs={{0,16},{16,0},{32,48},{48,32},{1,17},{17,1},{33,49},{49,33},{2,18}... | collective-permute-start | bytes 3145736 | tf_op jit(solution)/shard_map/ppermute | solution.py:46
  57.4 22.5 %all-to-all-start.1 = ((bf16[4,128,1408]{2,1,0:T(8,128)(2,1)}), bf16[4,128,1408]{2,1,0:T(8,128)(2,1)S(1)}, u32[]{:S(2)}, u32[]{:S(2)}) async-start(bf16[4,128,1408]{2,1,0:T(8,128)(2,1)} %shard_map.118), calls=%async_computation.1 | async-start | bytes 2883584 | tf_op jit(solution)/shard_map/all_to_all | solution.py:54
  73.3 14.0 %collective-permute-start.11 = (bf16[4,2,512,128]{3,2,1,0:T(8,128)(2,1)}, bf16[4,2,512,128]{3,2,1,0:T(8,128)(2,1)S(1)}, u32[]{:S(2)}, u32[]{:S(2)}) collective-permute-start(bf16[4,2,512,128]{3,2,1,0:T(8,128)(2,1)} %collective-permute-done.10.far_own), channel_id=1, source_target_pairs={{0,1},{1,0},{2,3},{3,2},{4,5},{5,4},{6,7},{7,6},{8,9},{9,8},{10,11... | collective-permute-start | bytes 3145736 | tf_op jit(solution)/shard_map/ppermute | solution.py:42
  81.0 1.3 collective-permute-start.9
  83.6 19.8 %all-to-all-start.2 = ((bf16[8,2,2,128,128]{4,3,2,1,0:T(8,128)(2,1)}), bf16[8,2,2,128,128]{4,3,2,1,0:T(8,128)(2,1)S(1)}, u32[]{:S(2)}, u32[]{:S(2)}) async-start(bf16[8,2,2,128,128]{4,3,2,1,0:T(8,128)(2,1)} %broadcast_in_dim.60), calls=%async_computation.2 | async-start | bytes 2097152 | tf_op jit(solution)/shard_map/all_to_all | solution.py:54
  98.4 1.0 copy-start.1
  99.3 25.4 %collective-permute-start.12 = (bf16[512,1024]{1,0:T(8,128)(2,1)}, bf16[512,1024]{1,0:T(8,128)(2,1)S(1)}, u32[]{:S(2)}, u32[]{:S(2)}) collective-permute-start(bf16[512,1024]{1,0:T(8,128)(2,1)} %fusion.1.own_ref), channel_id=1, source_target_pairs={{0,16},{16,0},{32,48},{48,32},{1,17},{17,1},{33,49},{49,33},{2,18}... | collective-permute-start | bytes 3145736 | tf_op jit(solution)/shard_map/ppermute | solution.py:46
  103.4 1.2 copy-start.2
  109.6 18.5 %all-to-all-start.3 = ((bf16[4,128,1024]{2,1,0:T(8,128)(2,1)}), bf16[4,128,1024]{2,1,0:T(8,128)(2,1)S(1)}, u32[]{:S(2)}, u32[]{:S(2)}) async-start(bf16[4,128,1024]{2,1,0:T(8,128)(2,1)} %broadcast_in_dim.61), calls=%async_computation.3 | async-start | bytes 2097152 | tf_op jit(solution)/shard_map/all_to_all | solution.py:54
  128.2 2.7 %collective-permute-start.13 = (bf16[512,1024]{1,0:T(8,128)(2,1)S(1)}, bf16[512,1024]{1,0:T(8,128)(2,1)S(1)}, u32[]{:S(2)}, u32[]{:S(2)}) collective-permute-start(bf16[512,1024]{1,0:T(8,128)(2,1)S(1)} %collective-permute-done.12.own_x_ref), channel_id=1, source_target_pairs={{0,1},{1,0},{2,3},{3,2},{4,5},{5,4},{6,7},{7,6},{8,9},{9,8},{10,11... | collective-permute-start | bytes 3145736 | tf_op jit(solution)/shard_map/ppermute | solution.py:42
  136.1 37.5 %all-to-all-start.4 = ((bf16[16,64,1024]{2,1,0:T(8,128)(2,1)}), bf16[16,64,1024]{2,1,0:T(8,128)(2,1)S(1)}, u32[]{:S(2)}, u32[]{:S(2)}) async-start(bf16[16,64,1024]{2,1,0:T(8,128)(2,1)} %bitcast.14), calls=%async_computation.4 | async-start | bytes 4194304 | tf_op jit(solution)/shard_map/all_to_all | solution.py:54
